TPU v7x, 32 devices: a whole 2x2x4 slice. The times are simulated.
32 devices in a mesh: dp: 32 (over z, y, x, core).
Axes of the slice: x: 2, y: 2, z: 4, core: 2. Of those that a mesh axis runs over, the one named last changes fastest.
Arguments:
- tokens: bfloat16 [100352, 768], P('dp'), may hold values from -6 to 6
- cotangent: bfloat16 [100352, 768], P('dp'), may hold values from -6 to 6
- skip_mask: int32 [512, 2], P('dp'), may hold values 0 or 1
- pair_index: int32 [512], P('dp'), may hold values from 0 to 511, as said below
- patch_up: bfloat16 [75264], P('dp'), may hold values from -0.4375 to 0.4375
- patch_down: bfloat16 [75264], P('dp'), may hold values from -0.3125 to 0.3125
- channel_up: bfloat16 [2359296], P('dp'), may hold values from -0.21875 to 0.21875
- channel_down: bfloat16 [2359296], P('dp'), may hold values from -0.109375 to 0.109375
- patch_upbias: bfloat16 [384], replicated, may hold values from -3 to 3
- patch_downbias: bfloat16 [196], replicated, may hold values from -3 to 3
- first_gain: bfloat16 [768], P('dp'), may hold values from 0.5 to 1.5
- first_shift: bfloat16 [768], P('dp'), may hold values from -3 to 3
- second_gain: bfloat16 [768], P('dp'), may hold values from 0.5 to 1.5
- second_shift: bfloat16 [768], P('dp'), may hold values from -3 to 3
- channel_upbias: bfloat16 [3072], P('dp'), may hold values from -3 to 3
- channel_downbias: bfloat16 [768], P('dp'), may hold values from -3 to 3
Outputs:
- mixed_out: bfloat16 [100352, 768], P('dp')
- pair_loss: float32 [512], P('dp')
- grad_tokens: float32 [100352, 768], P('dp')
- grad_patch_up: float32 [75264], P('dp')
- grad_patch_down: float32 [75264], P('dp')
- grad_channel_up: float32 [2359296], P('dp')
- grad_channel_down: float32 [2359296], P('dp')
- grad_patch_upbias: float32 [384], replicated
- grad_patch_downbias: float32 [196], replicated
- grad_first_gain: float32 [768], P('dp')
- grad_first_shift: float32 [768], P('dp')
- grad_second_gain: float32 [768], P('dp')
- grad_second_shift: float32 [768], P('dp')
- grad_channel_upbias: float32 [3072], P('dp')
- grad_channel_downbias: float32 [768], P('dp')
Inputs may be any that keep to these rules, and one draw needn't show every extreme that they name: pair_index[pair_index[c]] = c and pair_index[c] != c for every crop c.
All inputs are finite; a program needn't handle non-finite values. No bound on the sum of `skip_mask` on one device may be relied on, other than what follows from the above.
Results may differ from a plain program's by a relative error of at most 0.0075.
Values may be sent and summed in bfloat16 or wider, within the bound.
No kernel may reach another device: no remote copies, remote signals or barrier semaphores. Data moves between devices by JAX's collectives and lax.ppermute only.
A program may use at most 320 MiB of HBM per device.

v0:
```python
import functools

import jax
import jax.numpy as jnp
import numpy as np
from jax import lax
from jax.experimental import pallas as pl
from jax.experimental.pallas import tpu as pltpu
from jax.sharding import PartitionSpec as P

D = 768
S = 196
DS = 384
DC = 3072

GROUP = 4
TILE = GROUP * S
WIN = 208
STEP = 192
ONES = 16

eps_norm = 1e-06
keep_scale = 4.0 / 3.0
f32 = jnp.float32
bf16 = jnp.bfloat16
MIB = 1024 * 1024


def resident(shape):
    zeros = (0,) * len(shape)
    return pl.BlockSpec(shape, lambda *_: zeros, pipeline_mode=pl.Buffered(1))


def smem():
    return pl.BlockSpec(memory_space=pltpu.SMEM)


def anywhere():
    return pl.BlockSpec(memory_space=pl.ANY)


def call(kernel, after, in_specs, args, vmem, **rest):
    count = len(args)

    def body(*refs):
        kernel(*refs[:count], *refs[count + len(after) :])

    return pl.pallas_call(
        body,
        in_specs=list(in_specs) + [anywhere()] * len(after),
        compiler_params=pltpu.CompilerParams(vmem_limit_bytes=vmem * MIB),
        **rest,
    )(*args, *after)


def kept(skip, crop, branch):
    return skip[crop, branch].astype(f32) * keep_scale


def dot(a, b):
    return jnp.dot(a, b, preferred_element_type=f32)


def dot_nt(a, b):
    return lax.dot_general(a, b, (((1,), (1,)), ((), ())), preferred_element_type=f32)


def gelu_and_slope(z):
    phi = 0.5 * (1.0 + lax.erf(z * 0.7071067811865476))
    return z * phi, phi + z * jnp.exp(-0.5 * z * z) * 0.3989422804014327


def normalize(v):
    center = v - jnp.mean(v, axis=-1, keepdims=True)
    inv = lax.rsqrt(jnp.mean(center * center, axis=-1, keepdims=True) + eps_norm)
    return center * inv, inv


def join(values, axis, total):
    out, start = None, 0
    for v in values:
        pads = [(0, 0)] * v.ndim
        pads[axis] = (start, total - start - v.shape[axis])
        start += v.shape[axis]
        v = jnp.pad(v, pads)
        out = v if out is None else out + v
    return out


def per_row(values, shape, start=0):
    rows = lax.broadcasted_iota(jnp.int32, shape, 0) + start
    out = jnp.broadcast_to(values[GROUP - 1], shape)
    for c in range(GROUP - 2, -1, -1):
        out = jnp.where(rows < (c + 1) * S, values[c], out)
    return out


def crop_sum(read, c):
    lo, hi = c * S, (c + 1) * S
    base = c * STEP
    width = read(base, 8).shape[1]
    total = jnp.sum(read(base + 16, STEP - 16), axis=0, keepdims=True)
    for piece in (base, base + STEP):
        rows = lax.broadcasted_iota(jnp.int32, (16, width), 0) + piece
        ok = (rows >= lo) & (rows < hi)
        total += jnp.sum(jnp.where(ok, read(piece, 16), 0.0), axis=0, keepdims=True)
    return total


def window_matrix(c, shape):
    return jnp.where(
        lax.broadcasted_iota(jnp.int32, shape, 0) == lax.broadcasted_iota(jnp.int32, shape, 1) + 4 * c, 1.0, 0.0
    ).astype(bf16)


def token_forward_kernel(skip, x, wu, wd, bu, bd, vecs, x1_out, h2, act, slope, wu_out, wd_out, h1, x1, wut, wdt, bdt):
    i = pl.program_id(0)

    @pl.when(i == 0)
    def _():
        for c in range(GROUP):
            move = window_matrix(c, (WIN, S))
            wu_out[c] = dot(move, wu[...]).astype(bf16)
            wut[c] = lax.dot_general(
                wu[...], move, (((0,), (1,)), ((), ())), preferred_element_type=f32
            ).astype(bf16)
            wd_out[c] = dot_nt(wd[...], move).astype(bf16)
            wdt[c] = dot_nt(move, wd[...]).astype(bf16)
            bdt[c] = jnp.sum(move.astype(f32) * bd[...], axis=1, keepdims=True)

    tokens = x[...].astype(f32)
    normed, _ = normalize(tokens)
    h1[...] = (normed * vecs[0:1, :] + vecs[1:2, :]).astype(bf16)
    x1[...] = tokens

    def lift(c):
        return dot(wut[c], h1[pl.ds(c * STEP, WIN), :]) + bu[...]

    later = lift(0)
    for c in range(GROUP):
        lifted, later = later, lift(c + 1) if c + 1 < GROUP else None
        value, grad = gelu_and_slope(lifted)
        value = value.astype(bf16)
        act[c] = value
        slope[c] = grad.astype(bf16)
        mixed = dot(wdt[c], value) + bdt[c]
        x1[pl.ds(c * STEP, WIN), :] += kept(skip, i * GROUP + c, 0) * mixed
    x1_out[...] = x1[...].astype(bf16)
    normed, _ = normalize(x1[...])
    h2[...] = (normed * vecs[2:3, :] + vecs[3:4, :]).astype(bf16)


def token_forward(skip, x, wu, wd, bu, bd, vecs, after=()):
    rows = x.shape[0]
    crops = rows // S
    tile = pl.BlockSpec((TILE, D), lambda i: (i, 0))
    hidden = pl.BlockSpec((GROUP, DS, D), lambda i: (i, 0, 0))
    moved = [(GROUP, WIN, DS), (GROUP, DS, WIN)]
    return call(
        token_forward_kernel,
        after,
        [
            smem(),
            tile,
            resident((S, DS)),
            resident((DS, S)),
            resident((DS, 1)),
            resident((1, S)),
            resident((4, D)),
        ],
        (skip, x, wu, wd, bu, bd, vecs),
        vmem=50,
        grid=(rows // TILE,),
        out_specs=[tile, tile, hidden, hidden] + [pl.BlockSpec(m, lambda i: (0, 0, 0)) for m in moved],
        out_shape=[
            jax.ShapeDtypeStruct((rows, D), bf16),
            jax.ShapeDtypeStruct((rows, D), bf16),
            jax.ShapeDtypeStruct((crops, DS, D), bf16),
            jax.ShapeDtypeStruct((crops, DS, D), bf16),
        ]
        + [jax.ShapeDtypeStruct(m, bf16) for m in moved],
        scratch_shapes=[
            pltpu.VMEM((TILE, D), bf16),
            pltpu.VMEM((TILE, D), f32),
            pltpu.VMEM((GROUP, DS, WIN), bf16),
            pltpu.VMEM((GROUP, WIN, DS), bf16),
            pltpu.VMEM((GROUP, WIN, 1), f32),
        ],
        cost_estimate=pl.CostEstimate(
            flops=20 * rows * DS * D, bytes_accessed=rows * D * 12, transcendentals=0
        ),
        name="token_forward",
    )


def hidden_kernel(h2, up, bias, act_low, act_high, z_out, sums):
    i = pl.program_id(0)
    chunk = 512
    count = DC // chunk

    def hidden(j):
        cols = pl.ds(j * chunk, chunk)
        return dot(h2[...], up[:, cols]) + bias[:, cols]

    later = hidden(0)
    for j in range(count):
        cols = pl.ds(j * chunk, chunk)
        z, later = later, hidden(j + 1) if j + 1 < count else None
        z_out[:, cols] = z.astype(bf16)
        value = z * (0.5 * (1.0 + lax.erf(z * 0.7071067811865476)))
        half, k = divmod(j, count // 2)
        (act_low, act_high)[half][:, pl.ds(k * chunk, chunk)] = value.astype(bf16)
        for c in range(GROUP):
            sums[pl.ds(i * GROUP + c, 1), cols] = crop_sum(lambda a, n: value[a : a + n], c)


def hidden_forward(h2, up, bias, after=()):
    rows = h2.shape[0]
    grid = rows // TILE
    half = pl.BlockSpec((TILE, DC // 2), lambda i: (i, 0))
    return call(
        hidden_kernel,
        after,
        [pl.BlockSpec((TILE, D), lambda i: (i, 0)), resident((D, DC)), resident((1, DC))],
        (h2, up, bias),
        vmem=60,
        grid=(grid,),
        out_specs=[
            half,
            half,
            pl.BlockSpec((TILE, DC), lambda i: (i, 0)),
            pl.BlockSpec((grid * GROUP, DC), lambda i: (0, 0)),
        ],
        out_shape=[
            jax.ShapeDtypeStruct((rows, DC // 2), bf16),
            jax.ShapeDtypeStruct((rows, DC // 2), bf16),
            jax.ShapeDtypeStruct((rows, DC), bf16),
            jax.ShapeDtypeStruct((grid * GROUP, DC), f32),
        ],
        cost_estimate=pl.CostEstimate(
            flops=3 * rows * D * DC, bytes_accessed=rows * DC * 4, transcendentals=0
        ),
        name="hidden_forward",
    )


def output_kernel(skip, act_low, act_high, down, x1, bias, cotangent, out, scaled, pooled):
    i = pl.program_id(0)
    scale = per_row([kept(skip, i * GROUP + c, 1) for c in range(GROUP)], (TILE, 1))
    branch = dot(act_low[...], down[pl.ds(0, DC // 2), :]) + bias[...]
    branch += dot(act_high[...], down[pl.ds(DC // 2, DC // 2), :])
    y = x1[...].astype(f32) + scale * branch
    out[...] = y.astype(bf16)
    scaled[...] = (scale * cotangent[...].astype(f32)).astype(bf16)
    for c in range(GROUP):
        pooled[pl.ds(i * GROUP + c, 1), :] = crop_sum(lambda a, n: y[a : a + n], c) * (1.0 / S)


def output_forward(skip, act_low, act_high, down, x1, bias, cotangent, after=()):
    rows = x1.shape[0]
    grid = rows // TILE
    tile = pl.BlockSpec((TILE, D), lambda i: (i, 0))
    half = pl.BlockSpec((TILE, DC // 2), lambda i: (i, 0))
    return call(
        output_kernel,
        after,
        [smem(), half, half, resident((DC, D)), tile, resident((1, D)), tile],
        (skip, act_low, act_high, down, x1, bias, cotangent),
        vmem=60,
        grid=(grid,),
        out_specs=[tile, tile, pl.BlockSpec((grid * GROUP, D), lambda i: (0, 0))],
        out_shape=[
            jax.ShapeDtypeStruct((rows, D), bf16),
            jax.ShapeDtypeStruct((rows, D), bf16),
            jax.ShapeDtypeStruct((grid * GROUP, D), f32),
        ],
        cost_estimate=pl.CostEstimate(
            flops=2 * rows * D * DC, bytes_accessed=rows * DC * 2 + rows * D * 10, transcendentals=0
        ),
        name="output_forward",
    )


def lane_blocks(rows):
    count = max(rows // 768, 1)
    return [(k * 768, 768 if k < count - 1 else rows - 768 * (count - 1)) for k in range(count)]


def hidden_backward_kernel(
    skip, where, cotangent, differ, h2, down, z, gz, dw_own, dw_other, db, sums, grad, h2t
):
    j = pl.program_id(0)
    blocks = lane_blocks(h2.shape[0])

    @pl.when(j == 0)
    def _():
        total = jnp.zeros((1, D), f32)
        for i in range(cotangent.shape[0] // TILE):
            rows = pl.ds(i * TILE, TILE)
            scale = per_row([kept(skip, i * GROUP + c, 1) for c in range(GROUP)], (TILE, 1))
            shift = per_row([differ[pl.ds(i * GROUP + c, 1), :] for c in range(GROUP)], (TILE, D))
            value = (scale * (cotangent[rows, :].astype(f32) + (8.0 / S) * shift)).astype(bf16)
            grad[rows, :] = value
            total += jnp.sum(value.astype(f32), axis=0, keepdims=True)
        sums[...] = total
        square = (D, D)
        same = lax.broadcasted_iota(jnp.int32, square, 0) == lax.broadcasted_iota(jnp.int32, square, 1)
        eye = jnp.where(same, 1.0, 0.0).astype(bf16)
        for start, size in blocks:
            h2t[:, pl.ds(start, size)] = dot_nt(eye, h2[pl.ds(start, size), :]).astype(bf16)

    def first(b):
        start, size = blocks[b]
        return dot_nt(grad[pl.ds(start, size), :], down[...])

    dw = db_sum = None
    later = first(0)
    for b, (start, size) in enumerate(blocks):
        rows = pl.ds(start, size)
        part, later = later, first(b + 1) if b + 1 < len(blocks) else None
        hidden = z[rows, :].astype(f32)
        slope = (
            0.5 * (1.0 + lax.erf(hidden * 0.7071067811865476))
            + hidden * jnp.exp(-0.5 * hidden * hidden) * 0.3989422804014327
        )
        part = part * slope
        added = jnp.sum(part, axis=0, keepdims=True)
        db_sum = added if db_sum is None else db_sum + added
        part = part.astype(bf16)
        gz[rows, :] = part
        added = dot(h2t[:, rows], part)
        dw = added if dw is None else dw + added
    db[...] = db_sum
    unit = dw_own.shape[1]
    dw = dw.reshape(D // (2 * unit), 2, unit, dw.shape[1])
    dw_own[...] = jnp.where(where[0] == 0, dw[:, 0], dw[:, 1]).astype(bf16)
    dw_other[...] = jnp.where(where[0] == 0, dw[:, 1], dw[:, 0]).astype(bf16)


def hidden_backward(skip, core, cotangent, differ, h2, down, z, unit, after=()):
    rows = cotangent.shape[0]
    chunk = 512
    grads = (D // (2 * unit), unit)
    wide = pl.BlockSpec((rows, chunk), lambda j: (0, j))
    return call(
        hidden_backward_kernel,
        after,
        [
            smem(),
            smem(),
            resident((rows, D)),
            resident(differ.shape),
            resident((rows, D)),
            pl.BlockSpec((chunk, D), lambda j: (j, 0)),
            wide,
        ],
        (skip, jnp.reshape(core, (1,)).astype(jnp.int32), cotangent, differ, h2, down, z),
        vmem=52,
        grid=(DC // chunk,),
        out_specs=[
            wide,
            pl.BlockSpec(grads + (chunk,), lambda j: (0, 0, j)),
            pl.BlockSpec(grads + (chunk,), lambda j: (0, 0, j)),
            pl.BlockSpec((1, chunk), lambda j: (0, j)),
            pl.BlockSpec((1, D), lambda j: (0, 0)),
        ],
        out_shape=[
            jax.ShapeDtypeStruct((rows, DC), bf16),
            jax.ShapeDtypeStruct(grads + (DC,), bf16),
            jax.ShapeDtypeStruct(grads + (DC,), bf16),
            jax.ShapeDtypeStruct((1, DC), f32),
            jax.ShapeDtypeStruct((1, D), f32),
        ],
        scratch_shapes=[pltpu.VMEM((rows, D), bf16), pltpu.VMEM((D, rows), bf16)],
        cost_estimate=pl.CostEstimate(
            flops=4 * rows * D * DC, bytes_accessed=rows * DC * 4, transcendentals=0
        ),
        name="hidden_backward",
    )


def norm_back(grad, gain, normed, inv):
    scaled = grad * gain
    return inv * (
        scaled
        - jnp.mean(scaled, axis=-1, keepdims=True)
        - normed * jnp.mean(scaled * normed, axis=-1, keepdims=True)
    )


def last_backward_kernel(
    skip, gz, up, x1, cotangent, differ, x, act, slope, wd, wu, vecs, *rest, begin, first
):
    start, (out, dwd, dwu, sums, gh2, gx1, gv, h1, gh1) = rest[:-9], rest[-9:]
    i = pl.program_id(0)

    @pl.when(i == 0)
    def _():
        if first:
            dwd[...] = jnp.zeros_like(dwd)
            dwu[...] = jnp.zeros_like(dwu)
            sums[...] = jnp.zeros_like(sums)
        else:
            dwd[...] = start[1][...]
            dwu[...] = start[2][...]
            sums[...] = start[3][...]

    i += begin

    def add(row, value):
        sums[row : row + 1, :] += jnp.sum(value, axis=0, keepdims=True)

    block = TILE // 2
    for p in range(2):
        rows = pl.ds(p * block, block)
        gh2[rows, :] = dot_nt(gz[rows, :], up[...])
    normed_one, inv_one = normalize(x[...].astype(f32))
    h1[...] = (normed_one * vecs[0:1, :] + vecs[1:2, :]).astype(bf16)
    for p in range(2):
        rows = pl.ds(p * block, block)
        grad = gh2[rows, :]
        normed, inv = normalize(x1[rows, :].astype(f32))
        add(2, grad * normed)
        add(3, grad)
        shift = per_row(
            [differ[pl.ds(i * GROUP + c, 1), :] for c in range(GROUP)], (block, D), start=p * block
        )
        value = (
            cotangent[rows, :].astype(f32)
            + (8.0 / S) * shift
            + norm_back(grad, vecs[2:3, :], normed, inv)
        )
        gx1[rows, :] = value
        scale = per_row(
            [kept(skip, i * GROUP + c, 0) for c in range(GROUP)], (block, 1), start=p * block
        )
        gv[rows, :] = (scale * value).astype(bf16)

    gh1[...] = jnp.zeros_like(gh1)
    ones = jnp.ones((ONES, D), bf16)

    def back(c):
        return dot(wd[c], gv[pl.ds(c * STEP, WIN), :])

    later = back(0)
    for c in range(GROUP):
        rows = pl.ds(c * STEP, WIN)
        grad, later = later, back(c + 1) if c + 1 < GROUP else None
        dwd[c] += dot_nt(jnp.concatenate([act[c], ones], axis=0), gv[rows, :])
        gu = (grad * slope[c].astype(f32)).astype(bf16)
        dwu[c] += dot_nt(jnp.concatenate([h1[rows, :], ones], axis=0), gu)
        gh1[rows, :] += dot(wu[c], gu)
    grad = gh1[...]
    add(0, grad * normed_one)
    add(1, grad)
    out[...] = gx1[...] + norm_back(grad, vecs[0:1, :], normed_one, inv_one)


def last_backward(
    skip, gz, up, x1, cotangent, differ, x, act, slope, wd, wu, vecs, begin, count, before=None, after=()
):
    rows = x.shape[0]
    tile = pl.BlockSpec((TILE, D), lambda i: (i + begin, 0))
    hidden = pl.BlockSpec((GROUP, DS, D), lambda i: (i + begin, 0, 0))
    shapes = [(GROUP, DS + ONES, WIN), (GROUP, WIN + ONES, DS), (4, D)]
    extra = () if before is None else tuple(before)
    return call(
        functools.partial(last_backward_kernel, begin=begin, first=before is None),
        after,
        [
            smem(),
            pl.BlockSpec((TILE, DC), lambda i: (i + begin, 0)),
            resident((D, DC)),
            tile,
            tile,
            resident(differ.shape),
            tile,
            hidden,
            hidden,
            resident((GROUP, DS, WIN)),
            resident((GROUP, WIN, DS)),
            resident((4, D)),
        ]
        + ([] if before is None else [anywhere()] + [resident(s) for s in shapes]),
        (skip, gz, up, x1, cotangent, differ, x, act, slope, wd, wu, vecs) + extra,
        vmem=48,
        grid=(count,),
        out_specs=[
            tile,
            pl.BlockSpec(shapes[0], lambda i: (0, 0, 0)),
            pl.BlockSpec(shapes[1], lambda i: (0, 0, 0)),
            pl.BlockSpec(shapes[2], lambda i: (0, 0)),
        ],
        out_shape=[jax.ShapeDtypeStruct((rows, D), f32)] + [jax.ShapeDtypeStruct(s, f32) for s in shapes],
        scratch_shapes=[
            pltpu.VMEM((TILE, D), f32),
            pltpu.VMEM((TILE, D), f32),
            pltpu.VMEM((TILE, D), bf16),
            pltpu.VMEM((TILE, D), bf16),
            pltpu.VMEM((TILE, D), f32),
        ],
        input_output_aliases={} if before is None else {12: 0},
        cost_estimate=pl.CostEstimate(
            flops=count * TILE * (2 * D * DC + 20 * DS * D),
            bytes_accessed=count * TILE * (DC * 2 + D * 24),
            transcendentals=0,
        ),
        name="last_backward",
    )


def merge_kernel(where, low, high, low_in, high_in, sums, shift, *outs):
    i = pl.program_id(0)
    half = pl.num_programs(0) // 2
    *outs, over = outs
    over[...] = jnp.zeros_like(over)
    for k, out in enumerate(outs):
        place = where[1] ^ k
        added = dot(sums[place, 0], shift[...])
        own = jnp.where(i < half, low[place, 0], high[place, 0]).astype(f32)
        got = jnp.where(i < half, low_in[place], high_in[place]).astype(f32)
        out[0] = (own + got + added).astype(bf16)


def merge(core, at_xy, plane, low, high, low_in, high_in, sums, shift):
    half, _, rows, _ = low.shape
    steps = half // plane
    first = lambda i: jnp.minimum(i, steps - 1)
    second = lambda i: jnp.maximum(i - steps, 0)
    return pl.pallas_call(
        merge_kernel,
        grid_spec=pltpu.PrefetchScalarGridSpec(
            num_scalar_prefetch=1,
            grid=(2 * steps,),
            in_specs=[
                pl.BlockSpec((plane, 1, rows, D), lambda i, w: (first(i), w[0], 0, 0)),
                pl.BlockSpec((plane, 1, rows, D), lambda i, w: (second(i), w[0], 0, 0)),
                pl.BlockSpec((plane, rows, D), lambda i, w: (first(i), 0, 0)),
                pl.BlockSpec((plane, rows, D), lambda i, w: (second(i), 0, 0)),
                pl.BlockSpec((plane, 1) + sums.shape[2:], lambda i, w: (i, w[0], 0, 0)),
                pl.BlockSpec(shift.shape, lambda i, w: (0, 0)),
            ],
            out_specs=[pl.BlockSpec((1, rows, D), lambda i, w: (i, 0, 0))] * plane
            + [pl.BlockSpec((8, 128), lambda i, w: (0, 0))],
        ),
        out_shape=[jax.ShapeDtypeStruct((2 * steps, rows, D), bf16)] * plane
        + [jax.ShapeDtypeStruct((8, 128), f32)],
        compiler_params=pltpu.CompilerParams(vmem_limit_bytes=60 * MIB),
        name="merge",
    )(jnp.stack([core, at_xy]).astype(jnp.int32), low, high, low_in, high_in, sums, shift)


def place_kernel(where, *refs, pieces, side):
    out, held, sems = refs[-3:]
    kz = 2 * side
    copies = []
    for plane in range(kz):
        for k, (column, places) in enumerate(pieces):
            own, other = refs[2 * k], refs[2 * k + 1]
            rows, cols = own.shape[-2:]
            for index, (z, y, x) in enumerate(places):
                if z != plane:
                    continue
                chip = ((where[0] ^ z) * side + (where[1] ^ y)) * side + (where[2] ^ x)
                if rows % 16 == 0:
                    for ref, core in ((own, where[3]), (other, 1 - where[3])):
                        start = pl.multiple_of((chip * 2 + core) * rows, rows)
                        held[pl.ds(start, rows), pl.ds(column, cols)] = ref[index]
                else:
                    both = [own[index].astype(f32), other[index].astype(f32)]
                    low = jnp.where(where[3] == 0, both[0], both[1])
                    high = jnp.where(where[3] == 0, both[1], both[0])
                    start = pl.multiple_of(chip * 2 * rows, 2 * rows)
                    value = jnp.concatenate([low, high], axis=0).astype(bf16)
                    held[pl.ds(start, 2 * rows), pl.ds(column, cols)] = value
        size = held.shape[0] // kz
        part = pl.ds(pl.multiple_of((where[0] ^ plane) * size, size), size)
        copies.append(pltpu.make_async_copy(held.at[part], out.at[part], sems.at[plane]))
        copies[-1].start()
    for copy in copies:
        copy.wait()


def behind(value, *others):
    return lax.optimization_barrier((value,) + others)[0]


class Net:
    def __init__(self, n):
        chips = n // 2
        side = 1
        while 2 * side * side * side < chips:
            side *= 2
        if 2 * side * side * side != chips:
            raise ValueError("unknown slice")
        self.n, self.side, self.chips = n, side, chips
        self.core = [1]
        self.xy = [2 * k for k in range(1, side * side)]
        self.x = [2 * k for k in range(1, side)]
        self.y = [2 * side * k for k in range(1, side)]
        self.z = [2 * side * side * k for k in range(1, 2 * side)]
        self.me = lax.axis_index("dp")
        self.at_core = self.me % 2
        self.at_xy = (self.me // 2) % (side * side)
        self.at_x = (self.me // 2) % side
        self.at_y = (self.me // (2 * side)) % side
        self.at_z = self.me // (2 * side * side)

    def swap(self, value, offset):
        return lax.ppermute(value, "dp", [(i, i ^ offset) for i in range(self.n)])

    def spread(self, value, offsets):
        return jnp.stack([value] + [self.swap(value, o) for o in offsets])

    def gather_small(self, value, beside=(), chips=False):
        held = value
        order = np.array([0], np.int64)
        steps = []
        for k, offsets in enumerate((self.z, self.xy) if chips else (self.z, self.xy, self.core)):
            held = self.spread(held, offsets)
            if k < len(beside):
                held = behind(held, beside[k])
            steps.append(held)
            order = (np.array([0] + offsets)[:, None] + order[None, :]).reshape(-1)
        return held.reshape((-1,) + value.shape), order, steps

    def plane(self, stacked):
        side = self.side
        places = [(z, 0, 0) for z in range(2 * side)]
        out = [(stacked, places, 0)]
        for k, offset in enumerate(self.xy):
            y, x = divmod(k + 1, side)
            out.append((self.swap(stacked, offset), [(z, y, x) for z, _, _ in places], 0))
        return out

    def place(self, parts, others, after=()):
        side, kz = self.side, 2 * self.side
        rows = parts[0][0].shape[1]
        width = max(column + blocks.shape[2] for blocks, _, column in parts)
        pairs = [(blocks, other) for (blocks, _, _), other in zip(parts, others)]
        shape = (self.n * rows, width)
        if rows % 8 == 0:
            pieces = [(column, places) for _, places, column in parts]
            where = jnp.stack([self.at_z, self.at_y, self.at_x, self.at_core]).astype(jnp.int32)
            inputs = [v for pair in pairs for v in pair]
            return call(
                functools.partial(place_kernel, pieces=pieces, side=side),
                after,
                [smem()] + [pl.BlockSpec(memory_space=pltpu.VMEM)] * len(inputs),
                (where, *inputs),
                vmem=50,
                out_specs=anywhere(),
                out_shape=jax.ShapeDtypeStruct(shape, bf16),
                scratch_shapes=[pltpu.VMEM(shape, bf16), pltpu.SemaphoreType.DMA((kz,))],
                name="place",
            )
        columns = {}
        for (blocks, places, column), pair in zip(parts, pairs):
            columns.setdefault(column, []).extend(
                (core, place, pair[core][k]) for k, place in enumerate(places) for core in (0, 1)
            )
        out = []
        for column in sorted(columns):
            blocks = sorted(columns[column], key=lambda b: (b[1], b[0]))
            held = jnp.stack([b[2] for b in blocks]).reshape(kz, side, side, 2, rows, -1)
            for axis, at in enumerate((self.at_z, self.at_y, self.at_x, self.at_core)):
                held = jnp.take(held, jnp.arange(held.shape[axis]) ^ at, axis=axis)
            out.append(held.reshape(shape[0], -1))
        return jnp.concatenate(out, axis=1)

    def pick(self, value, index, axis):
        return lax.dynamic_index_in_dim(value, index, axis, keepdims=False)

    def start_axis(self, value, axis, at, offsets):
        own = self.pick(value, at, axis)
        return [own] + [
            self.swap(self.pick(value, at ^ (k + 1), axis).astype(bf16), o) for k, o in enumerate(offsets)
        ]

    def finish_axis(self, parts):
        parts = [p.astype(f32) for p in parts]
        while len(parts) > 1:
            parts = [parts[k] + parts[k + 1] for k in range(0, len(parts), 2)]
        return parts[0]

    def scatter_small(self, value):
        kz, k = 2 * self.side, self.side
        value = value.reshape(kz, k * k, 2, -1)
        value = self.finish_axis(self.start_axis(value, 2, self.at_core, self.core)).astype(bf16)
        value = self.finish_axis(self.start_axis(value, 1, self.at_xy, self.xy)).astype(bf16)
        return self.finish_axis(self.start_axis(value, 0, self.at_z, self.z))


def per_device(
    tokens,
    cotangent,
    skip_mask,
    pair_index,
    patch_up,
    patch_down,
    channel_up,
    channel_down,
    patch_upbias,
    patch_downbias,
    first_gain,
    first_shift,
    second_gain,
    second_shift,
    channel_upbias,
    channel_downbias,
    devices,
):
    net = Net(devices)
    chips = devices // 2
    core = net.at_core
    rows = tokens.shape[0]
    crops = rows // S
    unit_d = D // devices
    unit_h = DC // devices
    kz, kxy = 2 * net.side, net.side * net.side

    small = [
        patch_up, patch_down, first_gain, first_shift, second_gain, second_shift, channel_upbias, channel_downbias,
    ]
    sizes = [v.shape[0] for v in small]
    length = sum(sizes)
    padded = -(-length // 1024) * 1024
    packed = join(small, 0, padded)
    every, order, steps = net.gather_small(packed)
    channel_up = behind(channel_up, steps[0])
    skip_mask, pair_index, patch_upbias, patch_downbias = lax.optimization_barrier(
        (skip_mask, pair_index, patch_upbias, patch_downbias, steps[1])
    )[:4]
    in_order = (jnp.arange(devices)[:, None] ^ net.me) == jnp.asarray(order, jnp.int32)[None, :]
    every = dot(in_order.astype(bf16), every).astype(bf16)
    ends = np.cumsum([0] + sizes)
    up_token = every[:, : ends[1]].reshape(S, DS)
    down_token = every[:, ends[1] : ends[2]].reshape(DS, S)
    vecs = every[:, ends[2] : ends[6]].astype(f32).reshape(devices, 4, unit_d).transpose(1, 0, 2).reshape(4, D)
    bias_hidden = every[:, ends[6] : ends[7]].astype(f32).reshape(1, DC)
    bias_out = every[:, ends[7] : ends[8]].astype(f32).reshape(1, D)

    up_stack = net.spread(channel_up.reshape(unit_d, DC), net.z)
    down_stack = net.spread(behind(channel_down, up_stack).reshape(unit_h, D), net.z)
    up_parts = net.plane(up_stack)

    x1, h2, act_t, slope_t, up_pad, down_pad = token_forward(
        skip_mask,
        tokens,
        up_token,
        down_token,
        patch_upbias.astype(f32).reshape(DS, 1),
        patch_downbias.astype(f32).reshape(1, S),
        vecs,
        after=(up_stack, bias_hidden, bias_out),
    )
    up_parts = [(behind(blocks, h2, down_stack), places, column) for blocks, places, column in up_parts]
    up = net.place(up_parts, [net.swap(blocks, 1) for blocks, _, _ in up_parts])
    down_parts = net.plane(behind(down_stack, h2))
    other_pairs, other_skip = net.swap(pair_index, 1), net.swap(skip_mask[:, 1], 1)
    act_low, act_high, z, act_sums = hidden_forward(h2, up, bias_hidden)
    down_parts = [(behind(blocks, act_sums), places, column) for blocks, places, column in down_parts]
    down = net.place(down_parts, [net.swap(blocks, 1) for blocks, _, _ in down_parts])
    outputs, scaled, pooled = output_forward(skip_mask, act_low, act_high, down, x1, bias_out, cotangent)
    other_pairs, other_skip = behind(other_pairs, act_sums), behind(other_skip, act_sums)

    chip_sums = act_sums.astype(bf16)
    chip_sums = jnp.concatenate([chip_sums, net.swap(chip_sums, 1)]).T.reshape(chips, 2, unit_h, 2 * crops)

    def grad_down(act):
        value = lax.dot_general(act, scaled, (((0,), (0,)), ((), ())), preferred_element_type=f32)
        return value.astype(bf16).reshape(chips // 2, 2, unit_h, D)

    low, high = grad_down(act_low), grad_down(act_high)
    every, order, steps = net.gather_small(pooled.astype(bf16), beside=(low, high), chips=True)
    every = every.reshape(-1, D)
    every_other = net.swap(every, 1)
    low, high = behind(low, steps[1]), behind(high, steps[1])
    received = [net.swap(net.pick(v, 1 - core, 1), 1) for v in (low, high)]
    codes = (order[:, None] * crops + np.arange(crops)[None, :]).reshape(1, -1)
    flip = net.me.astype(jnp.int32) * crops

    def find(index):
        code = (index.reshape(-1, 1) ^ flip) - jnp.asarray(codes, jnp.int32)
        return dot((code == 0).astype(bf16), every) + dot((code == crops).astype(bf16), every_other)

    partner = find(jnp.stack([pair_index, other_pairs]))
    differ = pooled - partner[:crops]
    own_code = jnp.stack([net.me, net.me ^ 1]).astype(jnp.int32)[:, None] * crops + jnp.arange(crops, dtype=jnp.int32)
    chip_differ = find(own_code) - partner
    losses = 2.0 * jnp.sum(differ * differ, axis=1)

    chip_keep = jnp.stack([skip_mask[:, 1], other_skip]).astype(f32).reshape(-1, 1) * keep_scale
    chip_shift = (chip_keep * (8.0 / S) * chip_differ).astype(bf16)
    *down_sum, over = merge(core, net.at_xy, kxy, low, high, *received, chip_sums, chip_shift)
    down_parts = [down_sum[0]] + [net.swap(v, o) for v, o in zip(down_sum[1:], net.xy)]

    gz, up_own, up_other, grad_bias_hidden, grad_bias_out = hidden_backward(
        skip_mask, core, cotangent, differ, h2, down, z, unit_d, after=(over,)
    )
    down_sum = net.finish_axis(down_parts)
    up_other = net.swap(behind(up_other, down_sum), 1)
    down_parts = net.start_axis(down_sum, 0, net.at_z, net.z)
    tiles = rows // TILE
    cuts = (0, 1, tiles)
    passed = (
        skip_mask, gz, up, x1, cotangent, differ, tokens, act_t, slope_t, down_pad, up_pad, vecs
    )
    done = last_backward(*passed, cuts[0], cuts[1] - cuts[0], after=(down_sum,))
    up_sum = (up_own.astype(f32) + behind(up_other, done[3]).astype(f32)).astype(bf16)
    down_grad = net.finish_axis([behind(v, done[3]) for v in down_parts]).reshape(-1)
    up_parts = net.start_axis(up_sum.reshape(kz, kxy, unit_d, DC), 1, net.at_xy, net.xy)
    grad_tokens, dwd, dwu, sums = last_backward(
        *passed, cuts[1], cuts[2] - cuts[1], before=done, after=(up_sum, down_grad)
    )
    up_sum = net.finish_axis([behind(v, sums) for v in up_parts])
    dwd, dwu, sums, up_sum = lax.optimization_barrier((dwd, dwu, sums, up_sum))
    up_parts = net.start_axis(up_sum, 0, net.at_z, net.z)
    up_grad = net.finish_axis(up_parts).reshape(-1)

    grad_patch_up = sum(dwu[c, 4 * c : 4 * c + S] for c in range(GROUP))
    grad_patch_down = sum(dwd[c, :DS, 4 * c : 4 * c + S] for c in range(GROUP))
    bias_up = sum(dwu[c, WIN] for c in range(GROUP))
    bias_down = sum(dwd[c, DS, 4 * c : 4 * c + S] for c in range(GROUP))
    scattered = [
        grad_patch_up, grad_patch_down, sums[0], sums[1], sums[2], sums[3], grad_bias_hidden, grad_bias_out
    ]
    scattered = [v.reshape(devices, -1) for v in scattered]
    scattered += [jnp.broadcast_to(v, (devices,) + v.shape) for v in (bias_up, bias_down)]
    total = sum(v.shape[1] for v in scattered)
    scattered = join([v.astype(bf16) for v in scattered], 1, -(-total // 1024) * 1024)
    own = net.scatter_small(scattered)
    ends = np.cumsum([0] + sizes + [DS, S])
    grads = [own[a:b] for a, b in zip(ends[:-1], ends[1:])]
    return (
        outputs, losses, grad_tokens, grads[0], grads[1], up_grad, down_grad, grads[8], grads[9], *grads[2:8],
    )


def solution(mesh):
    row, flat, whole = P("dp", None), P("dp"), P()
    return jax.shard_map(
        functools.partial(per_device, devices=mesh.shape["dp"]),
        mesh=mesh,
        in_specs=(row, row, row, flat, flat, flat, flat, flat, whole, whole) + (flat,) * 6,
        out_specs=(row, flat, row, flat, flat, flat, flat, whole, whole) + (flat,) * 6,
        check_vma=False,
    )
```

profile of v0, /device:TPU:0, one launch (start us, length us, event | category | flops | bytes accessed | tf_op | source)
XLA Modules:
  0.0 336.7 jit_solution(15107506139498244621)
XLA Ops:
  1.6 3.1 collective-permute-start
  4.7 2.6 collective-permute-start.1
  7.3 1.9 collective-permute-done.1
  9.3 3.5 %collective-permute-done.2 = bf16[5120]{0:T(1024)(128)(2,1)S(1)} collective-permute-done((bf16[5120]{0:T(1024)(128)(2,1)S(1)}, bf16[5120]{0:T(1024)(128)(2,1)S(1)}, u32[]{:S(2)}, u32[]{:S(2)}) %collective-permute-start.2) | collective-permute-done | bytes 10272 | tf_op jit(solution)/shard_map/ppermute | solution.py:610
  12.9 1.6 collective-permute-start.3
  14.4 1.5 collective-permute-start.4
  18.7 4.3 %collective-permute-start.8 = (bf16[24,3072]{1,0:T(8,128)(2,1)S(1)}, bf16[24,3072]{1,0:T(8,128)(2,1)S(1)}, u32[]{:S(2)}, u32[]{:S(2)}) collective-permute-start(bf16[24,3072]{1,0:T(8,128)(2,1)S(1)} %reshape.217), channel_id=1, source_target_pairs={{0,16},{1,17},{2,18},{3,19},{4,20},{5,21},{6,22},{7,23},{8,24},{9,... | collective-permute-start | bytes 442376 | tf_op jit(solution)/shard_map/ppermute | solution.py:610
  25.7 4.6 %collective-permute-done.8 = bf16[24,3072]{1,0:T(8,128)(2,1)S(1)} collective-permute-done((bf16[24,3072]{1,0:T(8,128)(2,1)S(1)}, bf16[24,3072]{1,0:T(8,128)(2,1)S(1)}, u32[]{:S(2)}, u32[]{:S(2)}) %collective-permute-start.8) | collective-permute-done | bytes 147488 | tf_op jit(solution)/shard_map/ppermute | solution.py:610
  31.2 1.2 collective-permute-start.11
  32.4 3.2 collective-permute-start.12
  35.7 2.5 collective-permute-start.18
  41.3 22.4 %token_forward.1 = (bf16[3136,768]{1,0:T(8,128)(2,1)}, bf16[3136,768]{1,0:T(8,128)(2,1)}, bf16[16,384,768]{2,1,0:T(8,128)(2,1)}, bf16[16,384,768]{2,1,0:T(8,128)...) custom-call(s32[16,2]{1,0:T(8,128)S(1)} %copy.45.refs_0_, bf16[3136,768]{1,0:T(8,128)(2,1)} %refs_6_.5, ...), custom_call_target="tpu_custom_call" | custom-call | flops 18496880640 | bytes 28901376 | tf_op jit(solution)/shard_map/token_forward/pallas_call | solution.py:48
  66.8 2.4 collective-permute-start.25
  70.4 4.5 %place.2.refs_1_.refs_2_ = bf16[768,3072]{1,0:T(8,128)(2,1)} custom-call(s32[4]{0:T(128)S(1)} %pad_add_fusion.1.refs_0_, bf16[4,24,3072]{2,1,0:T(8,128)(2,1)S(1)} %pad_maximum_fusion.refs_7_.refs_1_, bf16[4,24,3072]{2,1,0:T(8,128)(2,1)} %collective-permute-done.13.refs_2_, bf16[4,24,3072]{2,1,0:T(8,128)(2,1)} %collective-permute-done.14.refs_3_, ...), custom_call_target="tpu_custom_call" | custom-call | tf_op jit(solution)/shard_map/place/pallas_call | solution.py:48
  74.9 27.9 %hidden_forward.1 = (bf16[3136,1536]{1,0:T(8,128)(2,1)}, bf16[3136,1536]{1,0:T(8,128)(2,1)}, bf16[3136,3072]{1,0:T(8,128)(2,1)}, f32[16,3072]{1,0:T(8,128)}) custom-call(bf16[3136,768]{1,0:T(8,128)(2,1)} %get-tuple-element.85.refs_0_.refs_4_, bf16[768,3072]{1,0:T(8,128)(2,1)} %place.2.refs_1_.refs_2_, f32[1,3072]{1,0:T(1,128)} %copy-done.3), custom_call_target="tpu_custom_call" | custom-call | flops 22196256768 | bytes 38535168 | tf_op jit(solution)/shard_map/hidden_forward/pallas_call | solution.py:48
  105.0 1.5 collective-permute-done.27
  107.9 1.1 collective-permute-done.37
  110.0 1.2 copy.46
  111.2 4.1 %place.3.refs_3_.refs_5_ = bf16[3072,768]{1,0:T(8,128)(2,1)} custom-call(s32[4]{0:T(128)S(1)} %pad_add_fusion.1.refs_0_, bf16[4,96,768]{2,1,0:T(8,128)(2,1)S(1)} %pad_maximum_fusion.1.refs_1_, bf16[4,96,768]{2,1,0:T(8,128)(2,1)} %collective-permute-done.20.refs_2_, bf16[4,96,768]{2,1,0:T(8,128)(2,1)} %collective-permute-done.21.refs_3_, ...), custom_call_target="tpu_custom_call" | custom-call | tf_op jit(solution)/shard_map/place/pallas_call | solution.py:48
  115.3 24.2 %output_forward.1 = (bf16[3136,768]{1,0:T(8,128)(2,1)}, bf16[3136,768]{1,0:T(8,128)(2,1)}, f32[16,768]{1,0:T(8,128)}) custom-call(s32[16,2]{1,0:T(8,128)} %copy-done.1, bf16[3136,1536]{1,0:T(8,128)(2,1)} %get-tuple-element.91.refs_1_, bf16[3136,1536]{1,0:T(8,128)(2,1)} %get-tuple-element.92.refs_2_, bf16[3072,768]{1,0:T(8,128)(2,1)} %place.3.refs_3_.refs_5_, ...), custom_call_target="tpu_custom_call" | custom-call | flops 14797504512 | bytes 43352064 | tf_op jit(solution)/shard_map/output_forward/pallas_call | solution.py:48
  141.4 3.3 collective-permute-start.30
  144.6 12.4 %convolution_convert_fusion.2 = bf16[1536,768]{1,0:T(8,128)(2,1)S(1)} fusion(bf16[3136,1536]{1,0:T(8,128)(2,1)} %get-tuple-element.91.refs_1_, bf16[3136,768]{1,0:T(8,128)(2,1)} %get-tuple-element.104), kind=kOutput, calls=%fused_computation.3 | convolution fusion | flops 7399931904 | bytes 16809984 | tf_op jit(solution)/shard_map/dot_general | solution.py:771
  157.1 1.5 collective-permute-start.31
  158.6 1.5 collective-permute-start.32
  160.7 11.0 %convolution_convert_fusion.1 = bf16[1536,768]{1,0:T(8,128)(2,1)S(1)} fusion(bf16[3136,1536]{1,0:T(8,128)(2,1)} %get-tuple-element.92.refs_2_, bf16[3136,768]{1,0:T(8,128)(2,1)S(1)} %copy-done.21), kind=kOutput, calls=%fused_computation.2 | convolution fusion | flops 7399931904 | bytes 16809984 | tf_op jit(solution)/shard_map/dot_general | solution.py:771
  175.3 1.7 collective-permute-done.35.low_in
  178.0 5.8 %merge.1 = (bf16[4,96,768]{2,1,0:T(8,128)(2,1)}, bf16[4,96,768]{2,1,0:T(8,128)(2,1)}, bf16[4,96,768]{2,1,0:T(8,128)(2,1)}, bf16[4,96,768]{2,1,0:T(8,128)(2,1)}, f32[8,128]{1,0:T(8,128)}) custom-call(s32[2]{0:T(128)} %pad_add_fusion.2.where, bf16[8,2,96,768]{3,2,1,0:T(8,128)(2,1)} %bitcast.117, bf16[8,2,96,768]{3,2,1,0:T(8,128)(2,1)} %bitcast.119, ...), custom_call_target="tpu_custom_call" | custom-call | tf_op jit(solution)/shard_map/merge/pallas_call | solution.py:530
  183.8 1.4 collective-permute-start.39
  185.2 1.5 collective-permute-start.40
  188.0 50.9 %hidden_backward.1 = (bf16[3136,3072]{1,0:T(8,128)(2,1)}, bf16[16,24,3072]{2,1,0:T(8,128)(2,1)}, bf16[16,24,3072]{2,1,0:T(8,128)(2,1)}, f32[1,3072]{1,0:T(1,128)S(1)}, f32[1,768]{1,0:T(1,128)S(1)}) custom-call(s32[16,2]{1,0:T(8,128)S(1)} %copy-done.2, s32[1]{0:T(128)} %bitcast.14.refs_1_, bf16[3136,768]{1,0:T(8,128)(2,1)} %refs_4_.3, ...), custom_call_target="tpu_custom_call" | custom-call | flops 29595009024 | bytes 38535168 | tf_op jit(solution)/shard_map/hidden_backward/pallas_call | solution.py:48
  239.8 1.1 collective-permute-start.44
  240.9 3.3 collective-permute-start.45
  244.2 16.3 %last_backward.2 = (f32[3136,768]{1,0:T(8,128)}, f32[4,400,208]{2,1,0:T(8,128)S(1)}, f32[4,224,384]{2,1,0:T(8,128)S(1)}, f32[4,768]{1,0:T(4,128)S(1)}) custom-call(s32[16,2]{1,0:T(8,128)S(1)} %copy-done.2, bf16[3136,3072]{1,0:T(8,128)(2,1)} %get-tuple-element.112.refs_1_, bf16[768,3072]{1,0:T(8,128)(2,1)} %place.2.refs_1_.refs_2_, ...), custom_call_target="tpu_custom_call" | custom-call | flops 8323596288 | bytes 19267584 | tf_op jit(solution)/shard_map/last_backward/pallas_call | solution.py:48
  260.5 1.2 copy-done.5
  263.0 3.4 add_convert_fusion.refs_16_
  266.6 1.2 copy-done.9
  267.8 1.4 collective-permute-start.46
  269.2 1.5 collective-permute-start.47
  271.3 35.7 %last_backward.3 = (f32[3136,768]{1,0:T(8,128)}, f32[4,400,208]{2,1,0:T(8,128)S(1)}, f32[4,224,384]{2,1,0:T(8,128)S(1)}, f32[4,768]{1,0:T(4,128)S(1)}) custom-call(s32[16,2]{1,0:T(8,128)S(1)} %copy-done.2, bf16[3136,3072]{1,0:T(8,128)(2,1)} %get-tuple-element.112.refs_1_, bf16[768,3072]{1,0:T(8,128)(2,1)} %place.2.refs_1_.refs_2_, ...), custom_call_target="tpu_custom_call", output_to_operand_aliasing={{0}: (12, {})} | custom-call | flops 24970788864 | bytes 57802752 | tf_op jit(solution)/shard_map/last_backward/pallas_call | solution.py:48
  312.7 1.5 collective-permute-start.50
  314.2 1.6 collective-permute-start.51
  316.6 1.1 collective-permute-start.57
  317.8 3.3 collective-permute-start.58
  321.4 1.1 collective-permute-start.54
  322.5 1.5 collective-permute-done.56
  324.0 1.8 collective-permute-start.55
  325.8 5.0 %collective-permute-done.57 = bf16[24,3072]{1,0:T(8,128)(2,1)S(1)} collective-permute-done((bf16[24,3072]{1,0:T(8,128)(2,1)S(1)}, bf16[24,3072]{1,0:T(8,128)(2,1)S(1)}, u32[]{:S(2)}, u32[]{:S(2)}) %collective-permute-start.57) | collective-permute-done | bytes 147488 | tf_op jit(solution)/shard_map/ppermute | solution.py:610
  331.6 1.5 collective-permute-done.54
  (228 shorter events, 41.0 us)
Async XLA Ops:
  1.6 5.7 %collective-permute-start = (bf16[5120]{0:T(1024)(128)(2,1)S(1)}, bf16[5120]{0:T(1024)(128)(2,1)S(1)}, u32[]{:S(2)}, u32[]{:S(2)}) collective-permute-start(bf16[5120]{0:T(1024)(128)(2,1)S(1)} %pad_add_fusion), channel_id=1, source_target_pairs={{0,8},{1,9},{2,10},{3,11},{4,12},{5,13},{6,14},{7,15},{8,0},{9,1},... | collective-permute-start | bytes 30728 | tf_op jit(solution)/shard_map/ppermute | solution.py:610
  7.3 5.5 %collective-permute-start.2 = (bf16[5120]{0:T(1024)(128)(2,1)S(1)}, bf16[5120]{0:T(1024)(128)(2,1)S(1)}, u32[]{:S(2)}, u32[]{:S(2)}) collective-permute-start(bf16[5120]{0:T(1024)(128)(2,1)S(1)} %pad_add_fusion), channel_id=1, source_target_pairs={{0,24},{1,25},{2,26},{3,27},{4,28},{5,29},{6,30},{7,31},{8,16},{9,... | collective-permute-start | bytes 30728 | tf_op jit(solution)/shard_map/ppermute | solution.py:610
  12.9 5.8 %collective-permute-start.3 = (bf16[4,5120]{1,0:T(4,128)(2,1)S(1)}, bf16[4,5120]{1,0:T(4,128)(2,1)S(1)}, u32[]{:S(2)}, u32[]{:S(2)}) collective-permute-start(bf16[4,5120]{1,0:T(4,128)(2,1)S(1)} %pad_maximum_fusion.6), channel_id=1, source_target_pairs={{0,2},{1,3},{2,0},{3,1},{4,6},{5,7},{6,4},{7,5},{8,10},{9,11},{10,... | collective-permute-start | bytes 122888 | tf_op jit(solution)/shard_map/ppermute | solution.py:610
  14.4 8.6 %collective-permute-start.4 = (bf16[4,5120]{1,0:T(4,128)(2,1)S(1)}, bf16[4,5120]{1,0:T(4,128)(2,1)S(1)}, u32[]{:S(2)}, u32[]{:S(2)}) collective-permute-start(bf16[4,5120]{1,0:T(4,128)(2,1)S(1)} %pad_maximum_fusion.6), channel_id=1, source_target_pairs={{0,4},{1,5},{2,6},{3,7},{4,0},{5,1},{6,2},{7,3},{8,12},{9,13},{10,... | collective-permute-start | bytes 122888 | tf_op jit(solution)/shard_map/ppermute | solution.py:610
  16.0 7.1 %collective-permute-start.5 = (bf16[4,5120]{1,0:T(4,128)(2,1)S(1)}, bf16[4,5120]{1,0:T(4,128)(2,1)S(1)}, u32[]{:S(2)}, u32[]{:S(2)}) collective-permute-start(bf16[4,5120]{1,0:T(4,128)(2,1)S(1)} %pad_maximum_fusion.6), channel_id=1, source_target_pairs={{0,6},{1,7},{2,4},{3,5},{4,2},{5,3},{6,0},{7,1},{8,14},{9,15},{10,... | collective-permute-start | bytes 122888 | tf_op jit(solution)/shard_map/ppermute | solution.py:610
  17.5 8.2 %collective-permute-start.9 = (bf16[24,3072]{1,0:T(8,128)(2,1)S(1)}, bf16[24,3072]{1,0:T(8,128)(2,1)S(1)}, u32[]{:S(2)}, u32[]{:S(2)}) collective-permute-start(bf16[24,3072]{1,0:T(8,128)(2,1)S(1)} %reshape.217), channel_id=1, source_target_pairs={{0,24},{1,25},{2,26},{3,27},{4,28},{5,29},{6,30},{7,31},{8,16},{9,... | collective-permute-start | bytes 442376 | tf_op jit(solution)/shard_map/ppermute | solution.py:610
  17.7 8.0 %collective-permute-start.7 = (bf16[24,3072]{1,0:T(8,128)(2,1)S(1)}, bf16[24,3072]{1,0:T(8,128)(2,1)S(1)}, u32[]{:S(2)}, u32[]{:S(2)}) collective-permute-start(bf16[24,3072]{1,0:T(8,128)(2,1)S(1)} %reshape.217), channel_id=1, source_target_pairs={{0,8},{1,9},{2,10},{3,11},{4,12},{5,13},{6,14},{7,15},{8,0},{9,1},... | collective-permute-start | bytes 442376 | tf_op jit(solution)/shard_map/ppermute | solution.py:610
  18.7 11.6 %collective-permute-start.8 = (bf16[24,3072]{1,0:T(8,128)(2,1)S(1)}, bf16[24,3072]{1,0:T(8,128)(2,1)S(1)}, u32[]{:S(2)}, u32[]{:S(2)}) collective-permute-start(bf16[24,3072]{1,0:T(8,128)(2,1)S(1)} %reshape.217), channel_id=1, source_target_pairs={{0,16},{1,17},{2,18},{3,19},{4,20},{5,21},{6,22},{7,23},{8,24},{9,... | collective-permute-start | bytes 442376 | tf_op jit(solution)/shard_map/ppermute | solution.py:610
  23.3 14.9 %collective-permute-start.6 = (bf16[4,4,5120]{2,1,0:T(4,128)(2,1)S(1)}, bf16[4,4,5120]{2,1,0:T(4,128)(2,1)S(1)}, u32[]{:S(2)}, u32[]{:S(2)}) collective-permute-start(bf16[4,4,5120]{2,1,0:T(4,128)(2,1)S(1)} %pad_maximum_fusion.4), channel_id=1, source_target_pairs={{0,1},{1,0},{2,3},{3,2},{4,5},{5,4},{6,7},{7,6},{8,9},{9,8},{10,11... | collective-permute-start | bytes 491528 | tf_op jit(solution)/shard_map/ppermute | solution.py:610
  31.2 9.5 %collective-permute-start.10 = (bf16[96,768]{1,0:T(8,128)(2,1)}, bf16[96,768]{1,0:T(8,128)(2,1)S(1)}, u32[]{:S(2)}, u32[]{:S(2)}) collective-permute-start(bf16[96,768]{1,0:T(8,128)(2,1)} %reshape.222), channel_id=1, source_target_pairs={{0,8},{1,9},{2,10},{3,11},{4,12},{5,13},{6,14},{7,15},{8,0},{9,1},... | collective-permute-start | bytes 442376 | tf_op jit(solution)/shard_map/ppermute | solution.py:610
  31.2 32.5 %collective-permute-start.11 = (bf16[96,768]{1,0:T(8,128)(2,1)}, bf16[96,768]{1,0:T(8,128)(2,1)}, u32[]{:S(2)}, u32[]{:S(2)}) collective-permute-start(bf16[96,768]{1,0:T(8,128)(2,1)} %reshape.222), channel_id=1, source_target_pairs={{0,16},{1,17},{2,18},{3,19},{4,20},{5,21},{6,22},{7,23},{8,24},{9,... | collective-permute-start | bytes 442376 | tf_op jit(solution)/shard_map/ppermute | solution.py:610
  32.4 31.3 %collective-permute-start.12 = (bf16[96,768]{1,0:T(8,128)(2,1)}, bf16[96,768]{1,0:T(8,128)(2,1)}, u32[]{:S(2)}, u32[]{:S(2)}) collective-permute-start(bf16[96,768]{1,0:T(8,128)(2,1)} %reshape.222), channel_id=1, source_target_pairs={{0,24},{1,25},{2,26},{3,27},{4,28},{5,29},{6,30},{7,31},{8,16},{9,... | collective-permute-start | bytes 442376 | tf_op jit(solution)/shard_map/ppermute | solution.py:610
  35.7 29.1 %collective-permute-start.18 = (bf16[4,24,3072]{2,1,0:T(8,128)(2,1)S(1)}, bf16[4,24,3072]{2,1,0:T(8,128)(2,1)}, u32[]{:S(2)}, u32[]{:S(2)}) collective-permute-start(bf16[4,24,3072]{2,1,0:T(8,128)(2,1)S(1)} %pad_maximum_fusion.refs_7_.refs_1_), channel_id=1, source_target_pairs={{0,6},{1,7},{2,4},{3,5},{4,2},{5,3},{6,0},{7,1},{8,14},{9,15},{10,... | collective-permute-start | bytes 1769480 | tf_op jit(solution)/shard_map/ppermute | solution.py:610
  38.2 27.1 %collective-permute-start.16 = (bf16[4,24,3072]{2,1,0:T(8,128)(2,1)S(1)}, bf16[4,24,3072]{2,1,0:T(8,128)(2,1)S(1)}, u32[]{:S(2)}, u32[]{:S(2)}) collective-permute-start(bf16[4,24,3072]{2,1,0:T(8,128)(2,1)S(1)} %pad_maximum_fusion.refs_7_.refs_1_), channel_id=1, source_target_pairs={{0,4},{1,5},{2,6},{3,7},{4,0},{5,1},{6,2},{7,3},{8,12},{9,13},{10,... | collective-permute-start | bytes 1769480 | tf_op jit(solution)/shard_map/ppermute | solution.py:610
  40.7 24.8 %collective-permute-start.14 = (bf16[4,24,3072]{2,1,0:T(8,128)(2,1)S(1)}, bf16[4,24,3072]{2,1,0:T(8,128)(2,1)}, u32[]{:S(2)}, u32[]{:S(2)}) collective-permute-start(bf16[4,24,3072]{2,1,0:T(8,128)(2,1)S(1)} %pad_maximum_fusion.refs_7_.refs_1_), channel_id=1, source_target_pairs={{0,2},{1,3},{2,0},{3,1},{4,6},{5,7},{6,4},{7,5},{8,10},{9,11},{10,... | collective-permute-start | bytes 1769480 | tf_op jit(solution)/shard_map/ppermute | solution.py:610
  65.4 5.0 %collective-permute-start.17 = (bf16[4,24,3072]{2,1,0:T(8,128)(2,1)S(1)}, bf16[4,24,3072]{2,1,0:T(8,128)(2,1)}, u32[]{:S(2)}, u32[]{:S(2)}) collective-permute-start(bf16[4,24,3072]{2,1,0:T(8,128)(2,1)S(1)} %collective-permute-done.16.refs_5_), channel_id=1, source_target_pairs={{0,1},{1,0},{2,3},{3,2},{4,5},{5,4},{6,7},{7,6},{8,9},{9,8},{10,11... | collective-permute-start | bytes 1769480 | tf_op jit(solution)/shard_map/ppermute | solution.py:610
  66.8 36.0 %collective-permute-start.25 = (bf16[4,96,768]{2,1,0:T(8,128)(2,1)S(1)}, bf16[4,96,768]{2,1,0:T(8,128)(2,1)}, u32[]{:S(2)}, u32[]{:S(2)}) collective-permute-start(bf16[4,96,768]{2,1,0:T(8,128)(2,1)S(1)} %pad_maximum_fusion.1.refs_1_), channel_id=1, source_target_pairs={{0,6},{1,7},{2,4},{3,5},{4,2},{5,3},{6,0},{7,1},{8,14},{9,15},{10,... | collective-permute-start | bytes 1769480 | tf_op jit(solution)/shard_map/ppermute | solution.py:610
  69.2 33.6 %collective-permute-start.23 = (bf16[4,96,768]{2,1,0:T(8,128)(2,1)S(1)}, bf16[4,96,768]{2,1,0:T(8,128)(2,1)}, u32[]{:S(2)}, u32[]{:S(2)}) collective-permute-start(bf16[4,96,768]{2,1,0:T(8,128)(2,1)S(1)} %pad_maximum_fusion.1.refs_1_), channel_id=1, source_target_pairs={{0,4},{1,5},{2,6},{3,7},{4,0},{5,1},{6,2},{7,3},{8,12},{9,13},{10,... | collective-permute-start | bytes 1769480 | tf_op jit(solution)/shard_map/ppermute | solution.py:610
  69.7 33.6 %collective-permute-start.21 = (bf16[4,96,768]{2,1,0:T(8,128)(2,1)S(1)}, bf16[4,96,768]{2,1,0:T(8,128)(2,1)}, u32[]{:S(2)}, u32[]{:S(2)}) collective-permute-start(bf16[4,96,768]{2,1,0:T(8,128)(2,1)S(1)} %pad_maximum_fusion.1.refs_1_), channel_id=1, source_target_pairs={{0,2},{1,3},{2,0},{3,1},{4,6},{5,7},{6,4},{7,5},{8,10},{9,11},{10,... | collective-permute-start | bytes 1769480 | tf_op jit(solution)/shard_map/ppermute | solution.py:610
  102.8 8.4 %collective-permute-start.26 = (bf16[4,96,768]{2,1,0:T(8,128)(2,1)}, bf16[4,96,768]{2,1,0:T(8,128)(2,1)}, u32[]{:S(2)}, u32[]{:S(2)}) collective-permute-start(bf16[4,96,768]{2,1,0:T(8,128)(2,1)} %collective-permute-done.25.refs_7_), channel_id=1, source_target_pairs={{0,1},{1,0},{2,3},{3,2},{4,5},{5,4},{6,7},{7,6},{8,9},{9,8},{10,11... | collective-permute-start | bytes 1769480 | tf_op jit(solution)/shard_map/ppermute | solution.py:610
  102.9 8.3 %collective-permute-start.24 = (bf16[4,96,768]{2,1,0:T(8,128)(2,1)}, bf16[4,96,768]{2,1,0:T(8,128)(2,1)S(1)}, u32[]{:S(2)}, u32[]{:S(2)}) collective-permute-start(bf16[4,96,768]{2,1,0:T(8,128)(2,1)} %collective-permute-done.23.refs_5_), channel_id=1, source_target_pairs={{0,1},{1,0},{2,3},{3,2},{4,5},{5,4},{6,7},{7,6},{8,9},{9,8},{10,11... | collective-permute-start | bytes 1769480 | tf_op jit(solution)/shard_map/ppermute | solution.py:610
  103.4 7.8 %collective-permute-start.22 = (bf16[4,96,768]{2,1,0:T(8,128)(2,1)}, bf16[4,96,768]{2,1,0:T(8,128)(2,1)S(1)}, u32[]{:S(2)}, u32[]{:S(2)}) collective-permute-start(bf16[4,96,768]{2,1,0:T(8,128)(2,1)} %collective-permute-done.21.refs_3_), channel_id=1, source_target_pairs={{0,1},{1,0},{2,3},{3,2},{4,5},{5,4},{6,7},{7,6},{8,9},{9,8},{10,11... | collective-permute-start | bytes 1769480 | tf_op jit(solution)/shard_map/ppermute | solution.py:610
  103.5 7.7 %collective-permute-start.20 = (bf16[4,96,768]{2,1,0:T(8,128)(2,1)S(1)}, bf16[4,96,768]{2,1,0:T(8,128)(2,1)}, u32[]{:S(2)}, u32[]{:S(2)}) collective-permute-start(bf16[4,96,768]{2,1,0:T(8,128)(2,1)S(1)} %pad_maximum_fusion.1.refs_1_), channel_id=1, source_target_pairs={{0,1},{1,0},{2,3},{3,2},{4,5},{5,4},{6,7},{7,6},{8,9},{9,8},{10,11... | collective-permute-start | bytes 1769480 | tf_op jit(solution)/shard_map/ppermute | solution.py:610
  140.2 16.8 %collective-permute-start.28 = (bf16[16,768]{1,0:T(8,128)(2,1)S(1)}, bf16[16,768]{1,0:T(8,128)(2,1)S(1)}, u32[]{:S(2)}, u32[]{:S(2)}) collective-permute-start(bf16[16,768]{1,0:T(8,128)(2,1)S(1)} %convert_element_type.260), channel_id=1, source_target_pairs={{0,8},{1,9},{2,10},{3,11},{4,12},{5,13},{6,14},{7,15},{8,0},{9,1},... | collective-permute-start | bytes 73736 | tf_op jit(solution)/shard_map/ppermute | solution.py:610
  140.3 16.8 %collective-permute-start.29 = (bf16[16,768]{1,0:T(8,128)(2,1)S(1)}, bf16[16,768]{1,0:T(8,128)(2,1)S(1)}, u32[]{:S(2)}, u32[]{:S(2)}) collective-permute-start(bf16[16,768]{1,0:T(8,128)(2,1)S(1)} %convert_element_type.260), channel_id=1, source_target_pairs={{0,16},{1,17},{2,18},{3,19},{4,20},{5,21},{6,22},{7,23},{8,24},{9,... | collective-permute-start | bytes 73736 | tf_op jit(solution)/shard_map/ppermute | solution.py:610
  141.4 15.7 %collective-permute-start.30 = (bf16[16,768]{1,0:T(8,128)(2,1)S(1)}, bf16[16,768]{1,0:T(8,128)(2,1)S(1)}, u32[]{:S(2)}, u32[]{:S(2)}) collective-permute-start(bf16[16,768]{1,0:T(8,128)(2,1)S(1)} %convert_element_type.260), channel_id=1, source_target_pairs={{0,24},{1,25},{2,26},{3,27},{4,28},{5,29},{6,30},{7,31},{8,16},{9,... | collective-permute-start | bytes 73736 | tf_op jit(solution)/shard_map/ppermute | solution.py:610
  157.1 14.6 %collective-permute-start.31 = (bf16[4,16,768]{2,1,0:T(8,128)(2,1)S(1)}, bf16[4,16,768]{2,1,0:T(8,128)(2,1)S(1)}, u32[]{:S(2)}, u32[]{:S(2)}) collective-permute-start(bf16[4,16,768]{2,1,0:T(8,128)(2,1)S(1)} %pad_maximum_fusion.5), channel_id=1, source_target_pairs={{0,2},{1,3},{2,0},{3,1},{4,6},{5,7},{6,4},{7,5},{8,10},{9,11},{10,... | collective-permute-start | bytes 294920 | tf_op jit(solution)/shard_map/ppermute | solution.py:610
  158.6 13.1 %collective-permute-start.32 = (bf16[4,16,768]{2,1,0:T(8,128)(2,1)S(1)}, bf16[4,16,768]{2,1,0:T(8,128)(2,1)S(1)}, u32[]{:S(2)}, u32[]{:S(2)}) collective-permute-start(bf16[4,16,768]{2,1,0:T(8,128)(2,1)S(1)} %pad_maximum_fusion.5), channel_id=1, source_target_pairs={{0,4},{1,5},{2,6},{3,7},{4,0},{5,1},{6,2},{7,3},{8,12},{9,13},{10,... | collective-permute-start | bytes 294920 | tf_op jit(solution)/shard_map/ppermute | solution.py:610
  160.1 11.6 %collective-permute-start.33 = (bf16[4,16,768]{2,1,0:T(8,128)(2,1)S(1)}, bf16[4,16,768]{2,1,0:T(8,128)(2,1)S(1)}, u32[]{:S(2)}, u32[]{:S(2)}) collective-permute-start(bf16[4,16,768]{2,1,0:T(8,128)(2,1)S(1)} %pad_maximum_fusion.5), channel_id=1, source_target_pairs={{0,6},{1,7},{2,4},{3,5},{4,2},{5,3},{6,0},{7,1},{8,14},{9,15},{10,... | collective-permute-start | bytes 294920 | tf_op jit(solution)/shard_map/ppermute | solution.py:610
  183.8 55.2 %collective-permute-start.39 = (bf16[4,96,768]{2,1,0:T(8,128)(2,1)}, bf16[4,96,768]{2,1,0:T(8,128)(2,1)S(1)}, u32[]{:S(2)}, u32[]{:S(2)}) collective-permute-start(bf16[4,96,768]{2,1,0:T(8,128)(2,1)} %get-tuple-element.118), channel_id=1, source_target_pairs={{0,2},{1,3},{2,0},{3,1},{4,6},{5,7},{6,4},{7,5},{8,10},{9,11},{10,... | collective-permute-start | bytes 1769480 | tf_op jit(solution)/shard_map/ppermute | solution.py:610
  185.2 53.7 %collective-permute-start.40 = (bf16[4,96,768]{2,1,0:T(8,128)(2,1)}, bf16[4,96,768]{2,1,0:T(8,128)(2,1)S(1)}, u32[]{:S(2)}, u32[]{:S(2)}) collective-permute-start(bf16[4,96,768]{2,1,0:T(8,128)(2,1)} %get-tuple-element.119), channel_id=1, source_target_pairs={{0,4},{1,5},{2,6},{3,7},{4,0},{5,1},{6,2},{7,3},{8,12},{9,13},{10,... | collective-permute-start | bytes 1769480 | tf_op jit(solution)/shard_map/ppermute | solution.py:610
  186.8 52.2 %collective-permute-start.41 = (bf16[4,96,768]{2,1,0:T(8,128)(2,1)}, bf16[4,96,768]{2,1,0:T(8,128)(2,1)S(1)}, u32[]{:S(2)}, u32[]{:S(2)}) collective-permute-start(bf16[4,96,768]{2,1,0:T(8,128)(2,1)} %get-tuple-element.120), channel_id=1, source_target_pairs={{0,6},{1,7},{2,4},{3,5},{4,2},{5,3},{6,0},{7,1},{8,14},{9,15},{10,... | collective-permute-start | bytes 1769480 | tf_op jit(solution)/shard_map/ppermute | solution.py:610
  239.3 23.7 %collective-permute-start.42 = (bf16[16,24,3072]{2,1,0:T(8,128)(2,1)}, bf16[16,24,3072]{2,1,0:T(8,128)(2,1)}, u32[]{:S(2)}, u32[]{:S(2)}) collective-permute-start(bf16[16,24,3072]{2,1,0:T(8,128)(2,1)} %get-tuple-element.127), channel_id=1, source_target_pairs={{0,1},{1,0},{2,3},{3,2},{4,5},{5,4},{6,7},{7,6},{8,9},{9,8},{10,11... | collective-permute-start | bytes 7077896 | tf_op jit(solution)/shard_map/ppermute | solution.py:610
  239.7 23.1 %collective-permute-start.43 = (bf16[96,768]{1,0:T(8,128)(2,1)S(1)}, bf16[96,768]{1,0:T(8,128)(2,1)S(1)}, u32[]{:S(2)}, u32[]{:S(2)}) collective-permute-start(bf16[96,768]{1,0:T(8,128)(2,1)S(1)} %get-tuple-element.163), channel_id=1, source_target_pairs={{0,8},{1,9},{2,10},{3,11},{4,12},{5,13},{6,14},{7,15},{8,0},{9,1},... | collective-permute-start | bytes 442376 | tf_op jit(solution)/shard_map/ppermute | solution.py:610
  239.8 23.1 %collective-permute-start.44 = (bf16[96,768]{1,0:T(8,128)(2,1)S(1)}, bf16[96,768]{1,0:T(8,128)(2,1)S(1)}, u32[]{:S(2)}, u32[]{:S(2)}) collective-permute-start(bf16[96,768]{1,0:T(8,128)(2,1)S(1)} %get-tuple-element.165), channel_id=1, source_target_pairs={{0,16},{1,17},{2,18},{3,19},{4,20},{5,21},{6,22},{7,23},{8,24},{9,... | collective-permute-start | bytes 442376 | tf_op jit(solution)/shard_map/ppermute | solution.py:610
  240.9 21.9 %collective-permute-start.45 = (bf16[96,768]{1,0:T(8,128)(2,1)S(1)}, bf16[96,768]{1,0:T(8,128)(2,1)S(1)}, u32[]{:S(2)}, u32[]{:S(2)}) collective-permute-start(bf16[96,768]{1,0:T(8,128)(2,1)S(1)} %get-tuple-element.164), channel_id=1, source_target_pairs={{0,24},{1,25},{2,26},{3,27},{4,28},{5,29},{6,30},{7,31},{8,16},{9,... | collective-permute-start | bytes 442376 | tf_op jit(solution)/shard_map/ppermute | solution.py:610
  267.8 39.2 %collective-permute-start.46 = (bf16[4,24,3072]{2,1,0:T(8,128)(2,1)S(1)}, bf16[4,24,3072]{2,1,0:T(8,128)(2,1)S(1)}, u32[]{:S(2)}, u32[]{:S(2)}) collective-permute-start(bf16[4,24,3072]{2,1,0:T(8,128)(2,1)S(1)} %get-tuple-element.159), channel_id=1, source_target_pairs={{0,2},{1,3},{2,0},{3,1},{4,6},{5,7},{6,4},{7,5},{8,10},{9,11},{10,... | collective-permute-start | bytes 1769480 | tf_op jit(solution)/shard_map/ppermute | solution.py:610
  269.2 37.9 %collective-permute-start.47 = (bf16[4,24,3072]{2,1,0:T(8,128)(2,1)S(1)}, bf16[4,24,3072]{2,1,0:T(8,128)(2,1)S(1)}, u32[]{:S(2)}, u32[]{:S(2)}) collective-permute-start(bf16[4,24,3072]{2,1,0:T(8,128)(2,1)S(1)} %get-tuple-element.158), channel_id=1, source_target_pairs={{0,4},{1,5},{2,6},{3,7},{4,0},{5,1},{6,2},{7,3},{8,12},{9,13},{10,... | collective-permute-start | bytes 1769480 | tf_op jit(solution)/shard_map/ppermute | solution.py:610
  270.7 36.3 %collective-permute-start.48 = (bf16[4,24,3072]{2,1,0:T(8,128)(2,1)S(1)}, bf16[4,24,3072]{2,1,0:T(8,128)(2,1)S(1)}, u32[]{:S(2)}, u32[]{:S(2)}) collective-permute-start(bf16[4,24,3072]{2,1,0:T(8,128)(2,1)S(1)} %get-tuple-element.157), channel_id=1, source_target_pairs={{0,6},{1,7},{2,4},{3,5},{4,2},{5,3},{6,0},{7,1},{8,14},{9,15},{10,... | collective-permute-start | bytes 1769480 | tf_op jit(solution)/shard_map/ppermute | solution.py:610
  312.7 5.0 %collective-permute-start.50 = (bf16[4,6144]{1,0:T(4,128)(2,1)S(1)}, bf16[4,6144]{1,0:T(4,128)(2,1)S(1)}, u32[]{:S(2)}, u32[]{:S(2)}) collective-permute-start(bf16[4,6144]{1,0:T(4,128)(2,1)S(1)} %bitcast.145), channel_id=1, source_target_pairs={{0,2},{1,3},{2,0},{3,1},{4,6},{5,7},{6,4},{7,5},{8,10},{9,11},{10,... | collective-permute-start | bytes 147464 | tf_op jit(solution)/shard_map/ppermute | solution.py:610
  314.2 6.8 %collective-permute-start.51 = (bf16[4,6144]{1,0:T(4,128)(2,1)S(1)}, bf16[4,6144]{1,0:T(4,128)(2,1)S(1)}, u32[]{:S(2)}, u32[]{:S(2)}) collective-permute-start(bf16[4,6144]{1,0:T(4,128)(2,1)S(1)} %bitcast.143), channel_id=1, source_target_pairs={{0,4},{1,5},{2,6},{3,7},{4,0},{5,1},{6,2},{7,3},{8,12},{9,13},{10,... | collective-permute-start | bytes 147464 | tf_op jit(solution)/shard_map/ppermute | solution.py:610
  315.9 5.2 %collective-permute-start.52 = (bf16[4,6144]{1,0:T(4,128)(2,1)S(1)}, bf16[4,6144]{1,0:T(4,128)(2,1)S(1)}, u32[]{:S(2)}, u32[]{:S(2)}) collective-permute-start(bf16[4,6144]{1,0:T(4,128)(2,1)S(1)} %bitcast.144), channel_id=1, source_target_pairs={{0,6},{1,7},{2,4},{3,5},{4,2},{5,3},{6,0},{7,1},{8,14},{9,15},{10,... | collective-permute-start | bytes 147464 | tf_op jit(solution)/shard_map/ppermute | solution.py:610
  316.6 7.5 %collective-permute-start.56 = (bf16[24,3072]{1,0:T(8,128)(2,1)S(1)}, bf16[24,3072]{1,0:T(8,128)(2,1)S(1)}, u32[]{:S(2)}, u32[]{:S(2)}) collective-permute-start(bf16[24,3072]{1,0:T(8,128)(2,1)S(1)} %get-tuple-element.160), channel_id=1, source_target_pairs={{0,8},{1,9},{2,10},{3,11},{4,12},{5,13},{6,14},{7,15},{8,0},{9,1},... | collective-permute-start | bytes 442376 | tf_op jit(solution)/shard_map/ppermute | solution.py:610
  316.6 14.1 %collective-permute-start.57 = (bf16[24,3072]{1,0:T(8,128)(2,1)S(1)}, bf16[24,3072]{1,0:T(8,128)(2,1)S(1)}, u32[]{:S(2)}, u32[]{:S(2)}) collective-permute-start(bf16[24,3072]{1,0:T(8,128)(2,1)S(1)} %get-tuple-element.162), channel_id=1, source_target_pairs={{0,16},{1,17},{2,18},{3,19},{4,20},{5,21},{6,22},{7,23},{8,24},{9,... | collective-permute-start | bytes 442376 | tf_op jit(solution)/shard_map/ppermute | solution.py:610
  317.8 13.0 %collective-permute-start.58 = (bf16[24,3072]{1,0:T(8,128)(2,1)S(1)}, bf16[24,3072]{1,0:T(8,128)(2,1)S(1)}, u32[]{:S(2)}, u32[]{:S(2)}) collective-permute-start(bf16[24,3072]{1,0:T(8,128)(2,1)S(1)} %get-tuple-element.161), channel_id=1, source_target_pairs={{0,24},{1,25},{2,26},{3,27},{4,28},{5,29},{6,30},{7,31},{8,16},{9,... | collective-permute-start | bytes 442376 | tf_op jit(solution)/shard_map/ppermute | solution.py:610
  321.3 10.3 %collective-permute-start.53 = (bf16[6144]{0:T(1024)(128)(2,1)S(1)}, bf16[6144]{0:T(1024)(128)(2,1)S(1)}, u32[]{:S(2)}, u32[]{:S(2)}) collective-permute-start(bf16[6144]{0:T(1024)(128)(2,1)S(1)} %get-tuple-element.147), channel_id=1, source_target_pairs={{0,8},{1,9},{2,10},{3,11},{4,12},{5,13},{6,14},{7,15},{8,0},{9,1},... | collective-permute-start | bytes 36872 | tf_op jit(solution)/shard_map/ppermute | solution.py:610
  321.4 11.7 %collective-permute-start.54 = (bf16[6144]{0:T(1024)(128)(2,1)S(1)}, bf16[6144]{0:T(1024)(128)(2,1)S(1)}, u32[]{:S(2)}, u32[]{:S(2)}) collective-permute-start(bf16[6144]{0:T(1024)(128)(2,1)S(1)} %get-tuple-element.149), channel_id=1, source_target_pairs={{0,16},{1,17},{2,18},{3,19},{4,20},{5,21},{6,22},{7,23},{8,24},{9,... | collective-permute-start | bytes 36872 | tf_op jit(solution)/shard_map/ppermute | solution.py:610
  324.0 9.1 %collective-permute-start.55 = (bf16[6144]{0:T(1024)(128)(2,1)S(1)}, bf16[6144]{0:T(1024)(128)(2,1)S(1)}, u32[]{:S(2)}, u32[]{:S(2)}) collective-permute-start(bf16[6144]{0:T(1024)(128)(2,1)S(1)} %get-tuple-element.148), channel_id=1, source_target_pairs={{0,24},{1,25},{2,26},{3,27},{4,28},{5,29},{6,30},{7,31},{8,16},{9,... | collective-permute-start | bytes 36872 | tf_op jit(solution)/shard_map/ppermute | solution.py:610
  (33 other events, 340.7 us)
where the time goes:
time: 341 us; the launch traced here: 337 us
  Pallas kernels  192 us (56%)
  starting transfers between devices  59.4 us (17%)
  matrix products  25.2 us (7%)
  waiting for transfers between devices  24.7 us (7%)
  local copies, waits for them, and re-layouts  20 us (6%)
  other arithmetic  13.6 us (4%)
    pallas_call x8, Pallas kernels, call(): pl.pallas_call(body, in_specs=list(in_specs) + [anywhere()] * len(after),...  186 us
    ppermute x59, starting transfers between devices, swap(): return lax.ppermute(value, 'dp', [(i, i ^ offset) for i in range(self.n)])  59.4 us
    ppermute x59, waiting for transfers between devices, swap(): return lax.ppermute(value, 'dp', [(i, i ^ offset) for i in range(self.n)])  24.7 us
    dot_general x2, matrix products, grad_down(): lax.dot_general(act, scaled, (((0,), (0,)), ((), ())), preferred_element_...  23.4 us
    unnamed x49, local copies, waits for them, and re-layouts  6.88 us
  transfers between devices with their start and end apart: 59, of which 13 were waited for; matrix products, arithmetic and copies ran while one was open for 12% of the time, Pallas kernels for 47%

commit v1 on v0

--- a/solution.py
+++ b/solution.py
@@ -811,7 +811,7 @@
     down_grad = net.finish_axis([behind(v, done[3]) for v in down_parts]).reshape(-1)
     up_parts = net.start_axis(up_sum.reshape(kz, kxy, unit_d, DC), 1, net.at_xy, net.xy)
     grad_tokens, dwd, dwu, sums = last_backward(
-        *passed, cuts[1], cuts[2] - cuts[1], before=done, after=(up_sum, down_grad)
+        *passed, cuts[1], cuts[2] - cuts[1], before=done, after=(down_grad,)
     )
     up_sum = net.finish_axis([behind(v, sums) for v in up_parts])
     dwd, dwu, sums, up_sum = lax.optimization_barrier((dwd, dwu, sums, up_sum))

time: 341 us -> 340 us (level)
    unnamed x49 -> x47, local copies, waits for them, and re-layouts: 6.88 us -> 5.7 us
where the time goes in v1:
time: 340 us; the launch traced here: 336 us
  Pallas kernels  192 us (56%)
  starting transfers between devices  59.4 us (17%)
  matrix products  25.3 us (7%)
  waiting for transfers between devices  24.7 us (7%)
  local copies, waits for them, and re-layouts  18.8 us (6%)
  other arithmetic  13.6 us (4%)
    pallas_call x8, Pallas kernels, call(): pl.pallas_call(body, in_specs=list(in_specs) + [anywhere()] * len(after),...  186 us
    ppermute x59, starting transfers between devices, swap(): return lax.ppermute(value, 'dp', [(i, i ^ offset) for i in range(self.n)])  59.4 us
    ppermute x59, waiting for transfers between devices, swap(): return lax.ppermute(value, 'dp', [(i, i ^ offset) for i in range(self.n)])  24.7 us
    dot_general x2, matrix products, grad_down(): lax.dot_general(act, scaled, (((0,), (0,)), ((), ())), preferred_element_...  23.5 us
  transfers between devices with their start and end apart: 59, of which 13 were waited for; matrix products, arithmetic and copies ran while one was open for 12% of the time, Pallas kernels for 47%

profile of v1, /device:TPU:0, one launch (start us, length us, event | category | flops | bytes accessed | tf_op | source)
XLA Modules:
  0.0 335.6 jit_solution(18127702446619403819)
XLA Ops:
  1.6 3.1 collective-permute-start
  4.7 2.6 collective-permute-start.1
  7.3 1.9 collective-permute-done.1
  9.3 3.5 %collective-permute-done.2 = bf16[5120]{0:T(1024)(128)(2,1)S(1)} collective-permute-done((bf16[5120]{0:T(1024)(128)(2,1)S(1)}, bf16[5120]{0:T(1024)(128)(2,1)S(1)}, u32[]{:S(2)}, u32[]{:S(2)}) %collective-permute-start.2) | collective-permute-done | bytes 10272 | tf_op jit(solution)/shard_map/ppermute | solution.py:610
  12.9 1.6 collective-permute-start.3
  14.4 1.5 collective-permute-start.4
  18.7 4.3 %collective-permute-start.8 = (bf16[24,3072]{1,0:T(8,128)(2,1)S(1)}, bf16[24,3072]{1,0:T(8,128)(2,1)S(1)}, u32[]{:S(2)}, u32[]{:S(2)}) collective-permute-start(bf16[24,3072]{1,0:T(8,128)(2,1)S(1)} %reshape.217), channel_id=1, source_target_pairs={{0,16},{1,17},{2,18},{3,19},{4,20},{5,21},{6,22},{7,23},{8,24},{9,... | collective-permute-start | bytes 442376 | tf_op jit(solution)/shard_map/ppermute | solution.py:610
  25.7 4.6 %collective-permute-done.8 = bf16[24,3072]{1,0:T(8,128)(2,1)S(1)} collective-permute-done((bf16[24,3072]{1,0:T(8,128)(2,1)S(1)}, bf16[24,3072]{1,0:T(8,128)(2,1)S(1)}, u32[]{:S(2)}, u32[]{:S(2)}) %collective-permute-start.8) | collective-permute-done | bytes 147488 | tf_op jit(solution)/shard_map/ppermute | solution.py:610
  31.2 1.2 collective-permute-start.11
  32.4 3.2 collective-permute-start.12
  35.7 2.5 collective-permute-start.18
  41.3 22.4 %token_forward.1 = (bf16[3136,768]{1,0:T(8,128)(2,1)}, bf16[3136,768]{1,0:T(8,128)(2,1)}, bf16[16,384,768]{2,1,0:T(8,128)(2,1)}, bf16[16,384,768]{2,1,0:T(8,128)...) custom-call(s32[16,2]{1,0:T(8,128)S(1)} %copy.45.refs_0_, bf16[3136,768]{1,0:T(8,128)(2,1)} %refs_6_.5, ...), custom_call_target="tpu_custom_call" | custom-call | flops 18496880640 | bytes 28901376 | tf_op jit(solution)/shard_map/token_forward/pallas_call | solution.py:48
  66.7 2.4 collective-permute-start.25
  70.3 4.5 %place.2.refs_1_.refs_2_ = bf16[768,3072]{1,0:T(8,128)(2,1)} custom-call(s32[4]{0:T(128)S(1)} %pad_add_fusion.1.refs_0_, bf16[4,24,3072]{2,1,0:T(8,128)(2,1)S(1)} %pad_maximum_fusion.refs_7_.refs_1_, bf16[4,24,3072]{2,1,0:T(8,128)(2,1)} %collective-permute-done.13.refs_2_, bf16[4,24,3072]{2,1,0:T(8,128)(2,1)} %collective-permute-done.14.refs_3_, ...), custom_call_target="tpu_custom_call" | custom-call | tf_op jit(solution)/shard_map/place/pallas_call | solution.py:48
  74.9 27.9 %hidden_forward.1 = (bf16[3136,1536]{1,0:T(8,128)(2,1)}, bf16[3136,1536]{1,0:T(8,128)(2,1)}, bf16[3136,3072]{1,0:T(8,128)(2,1)}, f32[16,3072]{1,0:T(8,128)}) custom-call(bf16[3136,768]{1,0:T(8,128)(2,1)} %get-tuple-element.85.refs_0_.refs_4_, bf16[768,3072]{1,0:T(8,128)(2,1)} %place.2.refs_1_.refs_2_, f32[1,3072]{1,0:T(1,128)} %copy-done.3), custom_call_target="tpu_custom_call" | custom-call | flops 22196256768 | bytes 38535168 | tf_op jit(solution)/shard_map/hidden_forward/pallas_call | solution.py:48
  105.0 1.5 collective-permute-done.27
  107.9 1.1 collective-permute-done.37
  109.9 1.2 copy.46
  111.2 4.1 %place.3.refs_3_.refs_5_ = bf16[3072,768]{1,0:T(8,128)(2,1)} custom-call(s32[4]{0:T(128)S(1)} %pad_add_fusion.1.refs_0_, bf16[4,96,768]{2,1,0:T(8,128)(2,1)S(1)} %pad_maximum_fusion.1.refs_1_, bf16[4,96,768]{2,1,0:T(8,128)(2,1)} %collective-permute-done.20.refs_2_, bf16[4,96,768]{2,1,0:T(8,128)(2,1)} %collective-permute-done.21.refs_3_, ...), custom_call_target="tpu_custom_call" | custom-call | tf_op jit(solution)/shard_map/place/pallas_call | solution.py:48
  115.2 24.2 %output_forward.1 = (bf16[3136,768]{1,0:T(8,128)(2,1)}, bf16[3136,768]{1,0:T(8,128)(2,1)}, f32[16,768]{1,0:T(8,128)}) custom-call(s32[16,2]{1,0:T(8,128)} %copy-done.1, bf16[3136,1536]{1,0:T(8,128)(2,1)} %get-tuple-element.91.refs_1_, bf16[3136,1536]{1,0:T(8,128)(2,1)} %get-tuple-element.92.refs_2_, bf16[3072,768]{1,0:T(8,128)(2,1)} %place.3.refs_3_.refs_5_, ...), custom_call_target="tpu_custom_call" | custom-call | flops 14797504512 | bytes 43352064 | tf_op jit(solution)/shard_map/output_forward/pallas_call | solution.py:48
  141.3 3.3 collective-permute-start.30
  144.6 12.4 %convolution_convert_fusion.2 = bf16[1536,768]{1,0:T(8,128)(2,1)S(1)} fusion(bf16[3136,1536]{1,0:T(8,128)(2,1)} %get-tuple-element.91.refs_1_, bf16[3136,768]{1,0:T(8,128)(2,1)} %get-tuple-element.104), kind=kOutput, calls=%fused_computation.3 | convolution fusion | flops 7399931904 | bytes 16809984 | tf_op jit(solution)/shard_map/dot_general | solution.py:771
  157.1 1.5 collective-permute-start.31
  158.6 1.5 collective-permute-start.32
  160.7 11.1 %convolution_convert_fusion.1 = bf16[1536,768]{1,0:T(8,128)(2,1)S(1)} fusion(bf16[3136,1536]{1,0:T(8,128)(2,1)} %get-tuple-element.92.refs_2_, bf16[3136,768]{1,0:T(8,128)(2,1)S(1)} %copy-done.20), kind=kOutput, calls=%fused_computation.2 | convolution fusion | flops 7399931904 | bytes 16809984 | tf_op jit(solution)/shard_map/dot_general | solution.py:771
  175.3 1.7 collective-permute-done.35.low_in
  178.0 5.8 %merge.1 = (bf16[4,96,768]{2,1,0:T(8,128)(2,1)}, bf16[4,96,768]{2,1,0:T(8,128)(2,1)}, bf16[4,96,768]{2,1,0:T(8,128)(2,1)}, bf16[4,96,768]{2,1,0:T(8,128)(2,1)}, f32[8,128]{1,0:T(8,128)}) custom-call(s32[2]{0:T(128)} %pad_add_fusion.2.where, bf16[8,2,96,768]{3,2,1,0:T(8,128)(2,1)} %bitcast.117, bf16[8,2,96,768]{3,2,1,0:T(8,128)(2,1)} %bitcast.119, ...), custom_call_target="tpu_custom_call" | custom-call | tf_op jit(solution)/shard_map/merge/pallas_call | solution.py:530
  183.8 1.4 collective-permute-start.39
  185.3 1.5 collective-permute-start.40
  188.0 50.9 %hidden_backward.1 = (bf16[3136,3072]{1,0:T(8,128)(2,1)}, bf16[16,24,3072]{2,1,0:T(8,128)(2,1)}, bf16[16,24,3072]{2,1,0:T(8,128)(2,1)}, f32[1,3072]{1,0:T(1,128)S(1)}, f32[1,768]{1,0:T(1,128)S(1)}) custom-call(s32[16,2]{1,0:T(8,128)S(1)} %copy-done.2, s32[1]{0:T(128)} %bitcast.14.refs_1_, bf16[3136,768]{1,0:T(8,128)(2,1)} %refs_4_.3, ...), custom_call_target="tpu_custom_call" | custom-call | flops 29595009024 | bytes 38535168 | tf_op jit(solution)/shard_map/hidden_backward/pallas_call | solution.py:48
  239.8 1.1 collective-permute-start.43
  240.9 3.3 collective-permute-start.44
  244.2 16.3 %last_backward.2 = (f32[3136,768]{1,0:T(8,128)}, f32[4,400,208]{2,1,0:T(8,128)S(1)}, f32[4,224,384]{2,1,0:T(8,128)S(1)}, f32[4,768]{1,0:T(4,128)S(1)}) custom-call(s32[16,2]{1,0:T(8,128)S(1)} %copy-done.2, bf16[3136,3072]{1,0:T(8,128)(2,1)} %get-tuple-element.112.refs_1_, bf16[768,3072]{1,0:T(8,128)(2,1)} %place.2.refs_1_.refs_2_, ...), custom_call_target="tpu_custom_call" | custom-call | flops 8323596288 | bytes 19267584 | tf_op jit(solution)/shard_map/last_backward/pallas_call | solution.py:48
  260.5 1.2 copy-done.5
  261.7 1.1 copy-done.6
  263.0 3.4 %add_convert_fusion = bf16[16,24,3072]{2,1,0:T(8,128)(2,1)S(1)} fusion(bf16[16,24,3072]{2,1,0:T(8,128)(2,1)} %collective-permute-done.45, bf16[16,24,3072]{2,1,0:T(8,128)(2,1)} %get-tuple-element.133), kind=kLoop, calls=%fused_computation.1 | loop fusion | flops 4718592 | bytes 7077888 | tf_op jit(solution)/shard_map/convert_element_type | solution.py:810
  266.6 1.5 collective-permute-start.46
  268.1 1.5 collective-permute-start.47
  270.2 35.7 %last_backward.3 = (f32[3136,768]{1,0:T(8,128)}, f32[4,400,208]{2,1,0:T(8,128)S(1)}, f32[4,224,384]{2,1,0:T(8,128)S(1)}, f32[4,768]{1,0:T(4,128)S(1)}) custom-call(s32[16,2]{1,0:T(8,128)S(1)} %copy-done.2, bf16[3136,3072]{1,0:T(8,128)(2,1)} %get-tuple-element.112.refs_1_, bf16[768,3072]{1,0:T(8,128)(2,1)} %place.2.refs_1_.refs_2_, ...), custom_call_target="tpu_custom_call", output_to_operand_aliasing={{0}: (12, {})} | custom-call | flops 24970788864 | bytes 57802752 | tf_op jit(solution)/shard_map/last_backward/pallas_call | solution.py:48
  311.6 1.5 collective-permute-start.50
  313.1 1.6 collective-permute-start.51
  315.5 1.1 collective-permute-start.57
  316.6 3.3 collective-permute-start.58
  320.3 1.1 collective-permute-start.54
  321.4 1.5 collective-permute-done.56
  322.9 1.8 collective-permute-start.55
  324.7 5.0 %collective-permute-done.57 = bf16[24,3072]{1,0:T(8,128)(2,1)S(1)} collective-permute-done((bf16[24,3072]{1,0:T(8,128)(2,1)S(1)}, bf16[24,3072]{1,0:T(8,128)(2,1)S(1)}, u32[]{:S(2)}, u32[]{:S(2)}) %collective-permute-start.57) | collective-permute-done | bytes 147488 | tf_op jit(solution)/shard_map/ppermute | solution.py:610
  330.5 1.5 collective-permute-done.54
  (226 shorter events, 39.8 us)
Async XLA Ops:
  1.6 5.7 %collective-permute-start = (bf16[5120]{0:T(1024)(128)(2,1)S(1)}, bf16[5120]{0:T(1024)(128)(2,1)S(1)}, u32[]{:S(2)}, u32[]{:S(2)}) collective-permute-start(bf16[5120]{0:T(1024)(128)(2,1)S(1)} %pad_add_fusion), channel_id=1, source_target_pairs={{0,8},{1,9},{2,10},{3,11},{4,12},{5,13},{6,14},{7,15},{8,0},{9,1},... | collective-permute-start | bytes 30728 | tf_op jit(solution)/shard_map/ppermute | solution.py:610
  7.3 5.5 %collective-permute-start.2 = (bf16[5120]{0:T(1024)(128)(2,1)S(1)}, bf16[5120]{0:T(1024)(128)(2,1)S(1)}, u32[]{:S(2)}, u32[]{:S(2)}) collective-permute-start(bf16[5120]{0:T(1024)(128)(2,1)S(1)} %pad_add_fusion), channel_id=1, source_target_pairs={{0,24},{1,25},{2,26},{3,27},{4,28},{5,29},{6,30},{7,31},{8,16},{9,... | collective-permute-start | bytes 30728 | tf_op jit(solution)/shard_map/ppermute | solution.py:610
  12.9 5.8 %collective-permute-start.3 = (bf16[4,5120]{1,0:T(4,128)(2,1)S(1)}, bf16[4,5120]{1,0:T(4,128)(2,1)S(1)}, u32[]{:S(2)}, u32[]{:S(2)}) collective-permute-start(bf16[4,5120]{1,0:T(4,128)(2,1)S(1)} %pad_maximum_fusion.6), channel_id=1, source_target_pairs={{0,2},{1,3},{2,0},{3,1},{4,6},{5,7},{6,4},{7,5},{8,10},{9,11},{10,... | collective-permute-start | bytes 122888 | tf_op jit(solution)/shard_map/ppermute | solution.py:610
  14.4 8.6 %collective-permute-start.4 = (bf16[4,5120]{1,0:T(4,128)(2,1)S(1)}, bf16[4,5120]{1,0:T(4,128)(2,1)S(1)}, u32[]{:S(2)}, u32[]{:S(2)}) collective-permute-start(bf16[4,5120]{1,0:T(4,128)(2,1)S(1)} %pad_maximum_fusion.6), channel_id=1, source_target_pairs={{0,4},{1,5},{2,6},{3,7},{4,0},{5,1},{6,2},{7,3},{8,12},{9,13},{10,... | collective-permute-start | bytes 122888 | tf_op jit(solution)/shard_map/ppermute | solution.py:610
  16.0 7.1 %collective-permute-start.5 = (bf16[4,5120]{1,0:T(4,128)(2,1)S(1)}, bf16[4,5120]{1,0:T(4,128)(2,1)S(1)}, u32[]{:S(2)}, u32[]{:S(2)}) collective-permute-start(bf16[4,5120]{1,0:T(4,128)(2,1)S(1)} %pad_maximum_fusion.6), channel_id=1, source_target_pairs={{0,6},{1,7},{2,4},{3,5},{4,2},{5,3},{6,0},{7,1},{8,14},{9,15},{10,... | collective-permute-start | bytes 122888 | tf_op jit(solution)/shard_map/ppermute | solution.py:610
  17.5 8.2 %collective-permute-start.9 = (bf16[24,3072]{1,0:T(8,128)(2,1)S(1)}, bf16[24,3072]{1,0:T(8,128)(2,1)S(1)}, u32[]{:S(2)}, u32[]{:S(2)}) collective-permute-start(bf16[24,3072]{1,0:T(8,128)(2,1)S(1)} %reshape.217), channel_id=1, source_target_pairs={{0,24},{1,25},{2,26},{3,27},{4,28},{5,29},{6,30},{7,31},{8,16},{9,... | collective-permute-start | bytes 442376 | tf_op jit(solution)/shard_map/ppermute | solution.py:610
  17.7 8.0 %collective-permute-start.7 = (bf16[24,3072]{1,0:T(8,128)(2,1)S(1)}, bf16[24,3072]{1,0:T(8,128)(2,1)S(1)}, u32[]{:S(2)}, u32[]{:S(2)}) collective-permute-start(bf16[24,3072]{1,0:T(8,128)(2,1)S(1)} %reshape.217), channel_id=1, source_target_pairs={{0,8},{1,9},{2,10},{3,11},{4,12},{5,13},{6,14},{7,15},{8,0},{9,1},... | collective-permute-start | bytes 442376 | tf_op jit(solution)/shard_map/ppermute | solution.py:610
  18.7 11.6 %collective-permute-start.8 = (bf16[24,3072]{1,0:T(8,128)(2,1)S(1)}, bf16[24,3072]{1,0:T(8,128)(2,1)S(1)}, u32[]{:S(2)}, u32[]{:S(2)}) collective-permute-start(bf16[24,3072]{1,0:T(8,128)(2,1)S(1)} %reshape.217), channel_id=1, source_target_pairs={{0,16},{1,17},{2,18},{3,19},{4,20},{5,21},{6,22},{7,23},{8,24},{9,... | collective-permute-start | bytes 442376 | tf_op jit(solution)/shard_map/ppermute | solution.py:610
  23.3 14.9 %collective-permute-start.6 = (bf16[4,4,5120]{2,1,0:T(4,128)(2,1)S(1)}, bf16[4,4,5120]{2,1,0:T(4,128)(2,1)S(1)}, u32[]{:S(2)}, u32[]{:S(2)}) collective-permute-start(bf16[4,4,5120]{2,1,0:T(4,128)(2,1)S(1)} %pad_maximum_fusion.4), channel_id=1, source_target_pairs={{0,1},{1,0},{2,3},{3,2},{4,5},{5,4},{6,7},{7,6},{8,9},{9,8},{10,11... | collective-permute-start | bytes 491528 | tf_op jit(solution)/shard_map/ppermute | solution.py:610
  31.2 9.5 %collective-permute-start.10 = (bf16[96,768]{1,0:T(8,128)(2,1)}, bf16[96,768]{1,0:T(8,128)(2,1)S(1)}, u32[]{:S(2)}, u32[]{:S(2)}) collective-permute-start(bf16[96,768]{1,0:T(8,128)(2,1)} %reshape.222), channel_id=1, source_target_pairs={{0,8},{1,9},{2,10},{3,11},{4,12},{5,13},{6,14},{7,15},{8,0},{9,1},... | collective-permute-start | bytes 442376 | tf_op jit(solution)/shard_map/ppermute | solution.py:610
  31.2 32.5 %collective-permute-start.11 = (bf16[96,768]{1,0:T(8,128)(2,1)}, bf16[96,768]{1,0:T(8,128)(2,1)}, u32[]{:S(2)}, u32[]{:S(2)}) collective-permute-start(bf16[96,768]{1,0:T(8,128)(2,1)} %reshape.222), channel_id=1, source_target_pairs={{0,16},{1,17},{2,18},{3,19},{4,20},{5,21},{6,22},{7,23},{8,24},{9,... | collective-permute-start | bytes 442376 | tf_op jit(solution)/shard_map/ppermute | solution.py:610
  32.4 31.3 %collective-permute-start.12 = (bf16[96,768]{1,0:T(8,128)(2,1)}, bf16[96,768]{1,0:T(8,128)(2,1)}, u32[]{:S(2)}, u32[]{:S(2)}) collective-permute-start(bf16[96,768]{1,0:T(8,128)(2,1)} %reshape.222), channel_id=1, source_target_pairs={{0,24},{1,25},{2,26},{3,27},{4,28},{5,29},{6,30},{7,31},{8,16},{9,... | collective-permute-start | bytes 442376 | tf_op jit(solution)/shard_map/ppermute | solution.py:610
  35.7 29.1 %collective-permute-start.18 = (bf16[4,24,3072]{2,1,0:T(8,128)(2,1)S(1)}, bf16[4,24,3072]{2,1,0:T(8,128)(2,1)}, u32[]{:S(2)}, u32[]{:S(2)}) collective-permute-start(bf16[4,24,3072]{2,1,0:T(8,128)(2,1)S(1)} %pad_maximum_fusion.refs_7_.refs_1_), channel_id=1, source_target_pairs={{0,6},{1,7},{2,4},{3,5},{4,2},{5,3},{6,0},{7,1},{8,14},{9,15},{10,... | collective-permute-start | bytes 1769480 | tf_op jit(solution)/shard_map/ppermute | solution.py:610
  38.2 27.1 %collective-permute-start.16 = (bf16[4,24,3072]{2,1,0:T(8,128)(2,1)S(1)}, bf16[4,24,3072]{2,1,0:T(8,128)(2,1)S(1)}, u32[]{:S(2)}, u32[]{:S(2)}) collective-permute-start(bf16[4,24,3072]{2,1,0:T(8,128)(2,1)S(1)} %pad_maximum_fusion.refs_7_.refs_1_), channel_id=1, source_target_pairs={{0,4},{1,5},{2,6},{3,7},{4,0},{5,1},{6,2},{7,3},{8,12},{9,13},{10,... | collective-permute-start | bytes 1769480 | tf_op jit(solution)/shard_map/ppermute | solution.py:610
  40.7 24.7 %collective-permute-start.14 = (bf16[4,24,3072]{2,1,0:T(8,128)(2,1)S(1)}, bf16[4,24,3072]{2,1,0:T(8,128)(2,1)}, u32[]{:S(2)}, u32[]{:S(2)}) collective-permute-start(bf16[4,24,3072]{2,1,0:T(8,128)(2,1)S(1)} %pad_maximum_fusion.refs_7_.refs_1_), channel_id=1, source_target_pairs={{0,2},{1,3},{2,0},{3,1},{4,6},{5,7},{6,4},{7,5},{8,10},{9,11},{10,... | collective-permute-start | bytes 1769480 | tf_op jit(solution)/shard_map/ppermute | solution.py:610
  65.3 5.0 %collective-permute-start.17 = (bf16[4,24,3072]{2,1,0:T(8,128)(2,1)S(1)}, bf16[4,24,3072]{2,1,0:T(8,128)(2,1)}, u32[]{:S(2)}, u32[]{:S(2)}) collective-permute-start(bf16[4,24,3072]{2,1,0:T(8,128)(2,1)S(1)} %collective-permute-done.16.refs_5_), channel_id=1, source_target_pairs={{0,1},{1,0},{2,3},{3,2},{4,5},{5,4},{6,7},{7,6},{8,9},{9,8},{10,11... | collective-permute-start | bytes 1769480 | tf_op jit(solution)/shard_map/ppermute | solution.py:610
  66.7 36.0 %collective-permute-start.25 = (bf16[4,96,768]{2,1,0:T(8,128)(2,1)S(1)}, bf16[4,96,768]{2,1,0:T(8,128)(2,1)}, u32[]{:S(2)}, u32[]{:S(2)}) collective-permute-start(bf16[4,96,768]{2,1,0:T(8,128)(2,1)S(1)} %pad_maximum_fusion.1.refs_1_), channel_id=1, source_target_pairs={{0,6},{1,7},{2,4},{3,5},{4,2},{5,3},{6,0},{7,1},{8,14},{9,15},{10,... | collective-permute-start | bytes 1769480 | tf_op jit(solution)/shard_map/ppermute | solution.py:610
  69.2 33.6 %collective-permute-start.23 = (bf16[4,96,768]{2,1,0:T(8,128)(2,1)S(1)}, bf16[4,96,768]{2,1,0:T(8,128)(2,1)}, u32[]{:S(2)}, u32[]{:S(2)}) collective-permute-start(bf16[4,96,768]{2,1,0:T(8,128)(2,1)S(1)} %pad_maximum_fusion.1.refs_1_), channel_id=1, source_target_pairs={{0,4},{1,5},{2,6},{3,7},{4,0},{5,1},{6,2},{7,3},{8,12},{9,13},{10,... | collective-permute-start | bytes 1769480 | tf_op jit(solution)/shard_map/ppermute | solution.py:610
  69.7 33.6 %collective-permute-start.21 = (bf16[4,96,768]{2,1,0:T(8,128)(2,1)S(1)}, bf16[4,96,768]{2,1,0:T(8,128)(2,1)}, u32[]{:S(2)}, u32[]{:S(2)}) collective-permute-start(bf16[4,96,768]{2,1,0:T(8,128)(2,1)S(1)} %pad_maximum_fusion.1.refs_1_), channel_id=1, source_target_pairs={{0,2},{1,3},{2,0},{3,1},{4,6},{5,7},{6,4},{7,5},{8,10},{9,11},{10,... | collective-permute-start | bytes 1769480 | tf_op jit(solution)/shard_map/ppermute | solution.py:610
  102.8 8.4 %collective-permute-start.26 = (bf16[4,96,768]{2,1,0:T(8,128)(2,1)}, bf16[4,96,768]{2,1,0:T(8,128)(2,1)}, u32[]{:S(2)}, u32[]{:S(2)}) collective-permute-start(bf16[4,96,768]{2,1,0:T(8,128)(2,1)} %collective-permute-done.25.refs_7_), channel_id=1, source_target_pairs={{0,1},{1,0},{2,3},{3,2},{4,5},{5,4},{6,7},{7,6},{8,9},{9,8},{10,11... | collective-permute-start | bytes 1769480 | tf_op jit(solution)/shard_map/ppermute | solution.py:610
  102.8 8.3 %collective-permute-start.24 = (bf16[4,96,768]{2,1,0:T(8,128)(2,1)}, bf16[4,96,768]{2,1,0:T(8,128)(2,1)S(1)}, u32[]{:S(2)}, u32[]{:S(2)}) collective-permute-start(bf16[4,96,768]{2,1,0:T(8,128)(2,1)} %collective-permute-done.23.refs_5_), channel_id=1, source_target_pairs={{0,1},{1,0},{2,3},{3,2},{4,5},{5,4},{6,7},{7,6},{8,9},{9,8},{10,11... | collective-permute-start | bytes 1769480 | tf_op jit(solution)/shard_map/ppermute | solution.py:610
  103.3 7.8 %collective-permute-start.22 = (bf16[4,96,768]{2,1,0:T(8,128)(2,1)}, bf16[4,96,768]{2,1,0:T(8,128)(2,1)S(1)}, u32[]{:S(2)}, u32[]{:S(2)}) collective-permute-start(bf16[4,96,768]{2,1,0:T(8,128)(2,1)} %collective-permute-done.21.refs_3_), channel_id=1, source_target_pairs={{0,1},{1,0},{2,3},{3,2},{4,5},{5,4},{6,7},{7,6},{8,9},{9,8},{10,11... | collective-permute-start | bytes 1769480 | tf_op jit(solution)/shard_map/ppermute | solution.py:610
  103.4 7.7 %collective-permute-start.20 = (bf16[4,96,768]{2,1,0:T(8,128)(2,1)S(1)}, bf16[4,96,768]{2,1,0:T(8,128)(2,1)}, u32[]{:S(2)}, u32[]{:S(2)}) collective-permute-start(bf16[4,96,768]{2,1,0:T(8,128)(2,1)S(1)} %pad_maximum_fusion.1.refs_1_), channel_id=1, source_target_pairs={{0,1},{1,0},{2,3},{3,2},{4,5},{5,4},{6,7},{7,6},{8,9},{9,8},{10,11... | collective-permute-start | bytes 1769480 | tf_op jit(solution)/shard_map/ppermute | solution.py:610
  140.2 16.8 %collective-permute-start.28 = (bf16[16,768]{1,0:T(8,128)(2,1)S(1)}, bf16[16,768]{1,0:T(8,128)(2,1)S(1)}, u32[]{:S(2)}, u32[]{:S(2)}) collective-permute-start(bf16[16,768]{1,0:T(8,128)(2,1)S(1)} %convert_element_type.260), channel_id=1, source_target_pairs={{0,8},{1,9},{2,10},{3,11},{4,12},{5,13},{6,14},{7,15},{8,0},{9,1},... | collective-permute-start | bytes 73736 | tf_op jit(solution)/shard_map/ppermute | solution.py:610
  140.2 16.8 %collective-permute-start.29 = (bf16[16,768]{1,0:T(8,128)(2,1)S(1)}, bf16[16,768]{1,0:T(8,128)(2,1)S(1)}, u32[]{:S(2)}, u32[]{:S(2)}) collective-permute-start(bf16[16,768]{1,0:T(8,128)(2,1)S(1)} %convert_element_type.260), channel_id=1, source_target_pairs={{0,16},{1,17},{2,18},{3,19},{4,20},{5,21},{6,22},{7,23},{8,24},{9,... | collective-permute-start | bytes 73736 | tf_op jit(solution)/shard_map/ppermute | solution.py:610
  141.3 15.8 %collective-permute-start.30 = (bf16[16,768]{1,0:T(8,128)(2,1)S(1)}, bf16[16,768]{1,0:T(8,128)(2,1)S(1)}, u32[]{:S(2)}, u32[]{:S(2)}) collective-permute-start(bf16[16,768]{1,0:T(8,128)(2,1)S(1)} %convert_element_type.260), channel_id=1, source_target_pairs={{0,24},{1,25},{2,26},{3,27},{4,28},{5,29},{6,30},{7,31},{8,16},{9,... | collective-permute-start | bytes 73736 | tf_op jit(solution)/shard_map/ppermute | solution.py:610
  157.1 14.6 %collective-permute-start.31 = (bf16[4,16,768]{2,1,0:T(8,128)(2,1)S(1)}, bf16[4,16,768]{2,1,0:T(8,128)(2,1)S(1)}, u32[]{:S(2)}, u32[]{:S(2)}) collective-permute-start(bf16[4,16,768]{2,1,0:T(8,128)(2,1)S(1)} %pad_maximum_fusion.5), channel_id=1, source_target_pairs={{0,2},{1,3},{2,0},{3,1},{4,6},{5,7},{6,4},{7,5},{8,10},{9,11},{10,... | collective-permute-start | bytes 294920 | tf_op jit(solution)/shard_map/ppermute | solution.py:610
  158.6 13.2 %collective-permute-start.32 = (bf16[4,16,768]{2,1,0:T(8,128)(2,1)S(1)}, bf16[4,16,768]{2,1,0:T(8,128)(2,1)S(1)}, u32[]{:S(2)}, u32[]{:S(2)}) collective-permute-start(bf16[4,16,768]{2,1,0:T(8,128)(2,1)S(1)} %pad_maximum_fusion.5), channel_id=1, source_target_pairs={{0,4},{1,5},{2,6},{3,7},{4,0},{5,1},{6,2},{7,3},{8,12},{9,13},{10,... | collective-permute-start | bytes 294920 | tf_op jit(solution)/shard_map/ppermute | solution.py:610
  160.1 11.7 %collective-permute-start.33 = (bf16[4,16,768]{2,1,0:T(8,128)(2,1)S(1)}, bf16[4,16,768]{2,1,0:T(8,128)(2,1)S(1)}, u32[]{:S(2)}, u32[]{:S(2)}) collective-permute-start(bf16[4,16,768]{2,1,0:T(8,128)(2,1)S(1)} %pad_maximum_fusion.5), channel_id=1, source_target_pairs={{0,6},{1,7},{2,4},{3,5},{4,2},{5,3},{6,0},{7,1},{8,14},{9,15},{10,... | collective-permute-start | bytes 294920 | tf_op jit(solution)/shard_map/ppermute | solution.py:610
  183.8 55.2 %collective-permute-start.39 = (bf16[4,96,768]{2,1,0:T(8,128)(2,1)}, bf16[4,96,768]{2,1,0:T(8,128)(2,1)S(1)}, u32[]{:S(2)}, u32[]{:S(2)}) collective-permute-start(bf16[4,96,768]{2,1,0:T(8,128)(2,1)} %get-tuple-element.118), channel_id=1, source_target_pairs={{0,2},{1,3},{2,0},{3,1},{4,6},{5,7},{6,4},{7,5},{8,10},{9,11},{10,... | collective-permute-start | bytes 1769480 | tf_op jit(solution)/shard_map/ppermute | solution.py:610
  185.3 53.7 %collective-permute-start.40 = (bf16[4,96,768]{2,1,0:T(8,128)(2,1)}, bf16[4,96,768]{2,1,0:T(8,128)(2,1)S(1)}, u32[]{:S(2)}, u32[]{:S(2)}) collective-permute-start(bf16[4,96,768]{2,1,0:T(8,128)(2,1)} %get-tuple-element.119), channel_id=1, source_target_pairs={{0,4},{1,5},{2,6},{3,7},{4,0},{5,1},{6,2},{7,3},{8,12},{9,13},{10,... | collective-permute-start | bytes 1769480 | tf_op jit(solution)/shard_map/ppermute | solution.py:610
  186.8 52.2 %collective-permute-start.41 = (bf16[4,96,768]{2,1,0:T(8,128)(2,1)}, bf16[4,96,768]{2,1,0:T(8,128)(2,1)S(1)}, u32[]{:S(2)}, u32[]{:S(2)}) collective-permute-start(bf16[4,96,768]{2,1,0:T(8,128)(2,1)} %get-tuple-element.120), channel_id=1, source_target_pairs={{0,6},{1,7},{2,4},{3,5},{4,2},{5,3},{6,0},{7,1},{8,14},{9,15},{10,... | collective-permute-start | bytes 1769480 | tf_op jit(solution)/shard_map/ppermute | solution.py:610
  239.3 23.7 %collective-permute-start.45 = (bf16[16,24,3072]{2,1,0:T(8,128)(2,1)}, bf16[16,24,3072]{2,1,0:T(8,128)(2,1)}, u32[]{:S(2)}, u32[]{:S(2)}) collective-permute-start(bf16[16,24,3072]{2,1,0:T(8,128)(2,1)} %get-tuple-element.135), channel_id=1, source_target_pairs={{0,1},{1,0},{2,3},{3,2},{4,5},{5,4},{6,7},{7,6},{8,9},{9,8},{10,11... | collective-permute-start | bytes 7077896 | tf_op jit(solution)/shard_map/ppermute | solution.py:610
  239.7 23.1 %collective-permute-start.42 = (bf16[96,768]{1,0:T(8,128)(2,1)S(1)}, bf16[96,768]{1,0:T(8,128)(2,1)S(1)}, u32[]{:S(2)}, u32[]{:S(2)}) collective-permute-start(bf16[96,768]{1,0:T(8,128)(2,1)S(1)} %get-tuple-element.163), channel_id=1, source_target_pairs={{0,8},{1,9},{2,10},{3,11},{4,12},{5,13},{6,14},{7,15},{8,0},{9,1},... | collective-permute-start | bytes 442376 | tf_op jit(solution)/shard_map/ppermute | solution.py:610
  239.8 23.1 %collective-permute-start.43 = (bf16[96,768]{1,0:T(8,128)(2,1)S(1)}, bf16[96,768]{1,0:T(8,128)(2,1)S(1)}, u32[]{:S(2)}, u32[]{:S(2)}) collective-permute-start(bf16[96,768]{1,0:T(8,128)(2,1)S(1)} %get-tuple-element.165), channel_id=1, source_target_pairs={{0,16},{1,17},{2,18},{3,19},{4,20},{5,21},{6,22},{7,23},{8,24},{9,... | collective-permute-start | bytes 442376 | tf_op jit(solution)/shard_map/ppermute | solution.py:610
  240.9 22.0 %collective-permute-start.44 = (bf16[96,768]{1,0:T(8,128)(2,1)S(1)}, bf16[96,768]{1,0:T(8,128)(2,1)S(1)}, u32[]{:S(2)}, u32[]{:S(2)}) collective-permute-start(bf16[96,768]{1,0:T(8,128)(2,1)S(1)} %get-tuple-element.164), channel_id=1, source_target_pairs={{0,24},{1,25},{2,26},{3,27},{4,28},{5,29},{6,30},{7,31},{8,16},{9,... | collective-permute-start | bytes 442376 | tf_op jit(solution)/shard_map/ppermute | solution.py:610
  266.6 39.3 %collective-permute-start.46 = (bf16[4,24,3072]{2,1,0:T(8,128)(2,1)S(1)}, bf16[4,24,3072]{2,1,0:T(8,128)(2,1)S(1)}, u32[]{:S(2)}, u32[]{:S(2)}) collective-permute-start(bf16[4,24,3072]{2,1,0:T(8,128)(2,1)S(1)} %get-tuple-element.159), channel_id=1, source_target_pairs={{0,2},{1,3},{2,0},{3,1},{4,6},{5,7},{6,4},{7,5},{8,10},{9,11},{10,... | collective-permute-start | bytes 1769480 | tf_op jit(solution)/shard_map/ppermute | solution.py:610
  268.1 37.8 %collective-permute-start.47 = (bf16[4,24,3072]{2,1,0:T(8,128)(2,1)S(1)}, bf16[4,24,3072]{2,1,0:T(8,128)(2,1)S(1)}, u32[]{:S(2)}, u32[]{:S(2)}) collective-permute-start(bf16[4,24,3072]{2,1,0:T(8,128)(2,1)S(1)} %get-tuple-element.158), channel_id=1, source_target_pairs={{0,4},{1,5},{2,6},{3,7},{4,0},{5,1},{6,2},{7,3},{8,12},{9,13},{10,... | collective-permute-start | bytes 1769480 | tf_op jit(solution)/shard_map/ppermute | solution.py:610
  269.6 36.3 %collective-permute-start.48 = (bf16[4,24,3072]{2,1,0:T(8,128)(2,1)S(1)}, bf16[4,24,3072]{2,1,0:T(8,128)(2,1)S(1)}, u32[]{:S(2)}, u32[]{:S(2)}) collective-permute-start(bf16[4,24,3072]{2,1,0:T(8,128)(2,1)S(1)} %get-tuple-element.157), channel_id=1, source_target_pairs={{0,6},{1,7},{2,4},{3,5},{4,2},{5,3},{6,0},{7,1},{8,14},{9,15},{10,... | collective-permute-start | bytes 1769480 | tf_op jit(solution)/shard_map/ppermute | solution.py:610
  311.6 5.0 %collective-permute-start.50 = (bf16[4,6144]{1,0:T(4,128)(2,1)S(1)}, bf16[4,6144]{1,0:T(4,128)(2,1)S(1)}, u32[]{:S(2)}, u32[]{:S(2)}) collective-permute-start(bf16[4,6144]{1,0:T(4,128)(2,1)S(1)} %bitcast.145), channel_id=1, source_target_pairs={{0,2},{1,3},{2,0},{3,1},{4,6},{5,7},{6,4},{7,5},{8,10},{9,11},{10,... | collective-permute-start | bytes 147464 | tf_op jit(solution)/shard_map/ppermute | solution.py:610
  313.1 6.8 %collective-permute-start.51 = (bf16[4,6144]{1,0:T(4,128)(2,1)S(1)}, bf16[4,6144]{1,0:T(4,128)(2,1)S(1)}, u32[]{:S(2)}, u32[]{:S(2)}) collective-permute-start(bf16[4,6144]{1,0:T(4,128)(2,1)S(1)} %bitcast.143), channel_id=1, source_target_pairs={{0,4},{1,5},{2,6},{3,7},{4,0},{5,1},{6,2},{7,3},{8,12},{9,13},{10,... | collective-permute-start | bytes 147464 | tf_op jit(solution)/shard_map/ppermute | solution.py:610
  314.7 5.1 %collective-permute-start.52 = (bf16[4,6144]{1,0:T(4,128)(2,1)S(1)}, bf16[4,6144]{1,0:T(4,128)(2,1)S(1)}, u32[]{:S(2)}, u32[]{:S(2)}) collective-permute-start(bf16[4,6144]{1,0:T(4,128)(2,1)S(1)} %bitcast.144), channel_id=1, source_target_pairs={{0,6},{1,7},{2,4},{3,5},{4,2},{5,3},{6,0},{7,1},{8,14},{9,15},{10,... | collective-permute-start | bytes 147464 | tf_op jit(solution)/shard_map/ppermute | solution.py:610
  315.4 7.5 %collective-permute-start.56 = (bf16[24,3072]{1,0:T(8,128)(2,1)S(1)}, bf16[24,3072]{1,0:T(8,128)(2,1)S(1)}, u32[]{:S(2)}, u32[]{:S(2)}) collective-permute-start(bf16[24,3072]{1,0:T(8,128)(2,1)S(1)} %get-tuple-element.160), channel_id=1, source_target_pairs={{0,8},{1,9},{2,10},{3,11},{4,12},{5,13},{6,14},{7,15},{8,0},{9,1},... | collective-permute-start | bytes 442376 | tf_op jit(solution)/shard_map/ppermute | solution.py:610
  315.5 14.1 %collective-permute-start.57 = (bf16[24,3072]{1,0:T(8,128)(2,1)S(1)}, bf16[24,3072]{1,0:T(8,128)(2,1)S(1)}, u32[]{:S(2)}, u32[]{:S(2)}) collective-permute-start(bf16[24,3072]{1,0:T(8,128)(2,1)S(1)} %get-tuple-element.162), channel_id=1, source_target_pairs={{0,16},{1,17},{2,18},{3,19},{4,20},{5,21},{6,22},{7,23},{8,24},{9,... | collective-permute-start | bytes 442376 | tf_op jit(solution)/shard_map/ppermute | solution.py:610
  316.6 13.0 %collective-permute-start.58 = (bf16[24,3072]{1,0:T(8,128)(2,1)S(1)}, bf16[24,3072]{1,0:T(8,128)(2,1)S(1)}, u32[]{:S(2)}, u32[]{:S(2)}) collective-permute-start(bf16[24,3072]{1,0:T(8,128)(2,1)S(1)} %get-tuple-element.161), channel_id=1, source_target_pairs={{0,24},{1,25},{2,26},{3,27},{4,28},{5,29},{6,30},{7,31},{8,16},{9,... | collective-permute-start | bytes 442376 | tf_op jit(solution)/shard_map/ppermute | solution.py:610
  320.2 10.3 %collective-permute-start.53 = (bf16[6144]{0:T(1024)(128)(2,1)S(1)}, bf16[6144]{0:T(1024)(128)(2,1)S(1)}, u32[]{:S(2)}, u32[]{:S(2)}) collective-permute-start(bf16[6144]{0:T(1024)(128)(2,1)S(1)} %get-tuple-element.147), channel_id=1, source_target_pairs={{0,8},{1,9},{2,10},{3,11},{4,12},{5,13},{6,14},{7,15},{8,0},{9,1},... | collective-permute-start | bytes 36872 | tf_op jit(solution)/shard_map/ppermute | solution.py:610
  320.3 11.7 %collective-permute-start.54 = (bf16[6144]{0:T(1024)(128)(2,1)S(1)}, bf16[6144]{0:T(1024)(128)(2,1)S(1)}, u32[]{:S(2)}, u32[]{:S(2)}) collective-permute-start(bf16[6144]{0:T(1024)(128)(2,1)S(1)} %get-tuple-element.149), channel_id=1, source_target_pairs={{0,16},{1,17},{2,18},{3,19},{4,20},{5,21},{6,22},{7,23},{8,24},{9,... | collective-permute-start | bytes 36872 | tf_op jit(solution)/shard_map/ppermute | solution.py:610
  322.9 9.1 %collective-permute-start.55 = (bf16[6144]{0:T(1024)(128)(2,1)S(1)}, bf16[6144]{0:T(1024)(128)(2,1)S(1)}, u32[]{:S(2)}, u32[]{:S(2)}) collective-permute-start(bf16[6144]{0:T(1024)(128)(2,1)S(1)} %get-tuple-element.148), channel_id=1, source_target_pairs={{0,24},{1,25},{2,26},{3,27},{4,28},{5,29},{6,30},{7,31},{8,16},{9,... | collective-permute-start | bytes 36872 | tf_op jit(solution)/shard_map/ppermute | solution.py:610
  (32 other events, 337.0 us)
